TPU v7x, 32 devices: a whole 2x2x4 slice. The times are simulated.
32 devices in a mesh: row: 8 (over y, x, core), col: 4 (over z).
Axes of the slice: x: 2, y: 2, z: 4, core: 2. Of those that a mesh axis runs over, the one named last changes fastest.
Arguments:
- trailing_in: float32 [2, 8, 256, 4, 4, 256], P(None, 'row', None, None, 'col'), may hold values from 0 to 4, as said below
Outputs:
- factored: float32 [2, 8, 256, 4, 4, 256], P(None, 'row', None, None, 'col')
Inputs may be any that keep to these rules, and one draw needn't show every extreme that they name: `trailing_in`: the matrix is symmetric and positive definite.
All inputs are finite; a program needn't handle non-finite values.
Results may differ from a plain program's by a relative error of at most 0.0003.
Values sent between devices are 32-bit elements; how exact they have to be, the bound alone decides.
No kernel may reach another device: no remote copies, remote signals or barrier semaphores. Data moves between devices by JAX's collectives and lax.ppermute only.
A program may use at most 64 MiB of HBM per device.

v0:
```python
import functools

import jax
import jax.numpy as jnp
from jax import lax
from jax.experimental import pallas as pl
from jax.experimental.pallas import tpu as pltpu
from jax.sharding import PartitionSpec as P

NB = 256
HALF = 128
SUB = 8
HIGHEST = lax.Precision.HIGHEST
HIGH = lax.Precision.HIGH


def mm(a, b, precision=HIGHEST):
    return lax.dot_general(
        a, b, (((1,), (0,)), ((), ())), precision=precision, preferred_element_type=jnp.float32
    )


def mm_t(a, b, precision=HIGHEST):
    return lax.dot_general(
        a, b, (((1,), (1,)), ((), ())), precision=precision, preferred_element_type=jnp.float32
    )


def t_mm(a, b, precision=HIGHEST):
    return lax.dot_general(
        a, b, (((0,), (0,)), ((), ())), precision=precision, preferred_element_type=jnp.float32
    )


def spread(x):
    return jnp.broadcast_to(x, (SUB, HALF))


def factor_half(s):
    groups = HALF // SUB
    lane = lax.broadcasted_iota(jnp.int32, (SUB, HALF), 1)
    sub = lax.broadcasted_iota(jnp.int32, (SUB, HALF), 0)
    rows = [s[SUB * g : SUB * (g + 1), :] for g in range(groups)]
    own_diagonal = [jnp.where(lane == sub + SUB * g, rows[g], 0.0) for g in range(groups)]
    diagonal = spread(jnp.sum(sum(own_diagonal), axis=0, keepdims=True))
    scale = lax.rsqrt(diagonal)
    unscale = diagonal * scale
    eyes = []
    for g in range(groups):
        down = spread(lax.rsqrt(jnp.sum(own_diagonal[g], axis=1, keepdims=True)))
        rows[g] = (rows[g] * scale) * down
        eyes.append(jnp.where(lane == sub + SUB * g, 1.0, 0.0).astype(jnp.float32))
    out_u, out_x = [], []
    for g in range(groups):
        base = SUB * g
        own = rows[g]
        own_x = eyes[g]
        a = {}
        for j in range(SUB):
            column = spread(own[:, base + j : base + j + 1])
            for i in range(j + 1):
                a[i, j] = spread(column[i : i + 1, :])
        near = None
        if g + 1 < groups:
            near = [spread(rows[g + 1][:, base + j : base + j + 1]) for j in range(SUB)]
        u = [spread(own[i : i + 1, :]) for i in range(SUB)]
        x = [spread(own_x[i : i + 1, :]) for i in range(SUB)]
        r = [None] * SUB
        l = {}
        for k in range(0, SUB, 2):
            p, q, t = a[k, k], a[k, k + 1], a[k + 1, k + 1]
            r[k] = lax.rsqrt(p)
            root = lax.rsqrt(p * t - q * q)
            both = r[k] * root
            r[k + 1] = (p * r[k]) * root
            l[k, k + 1] = q * r[k]
            for j in range(k + 2, SUB):
                l[k, j] = a[k, j] * r[k]
                l[k + 1, j] = (p * a[k + 1, j] - q * a[k, j]) * both
            for i in range(k + 2, SUB):
                for j in range(i, SUB):
                    a[i, j] = (a[i, j] - l[k, i] * l[k, j]) - l[k + 1, i] * l[k + 1, j]
            for m in (k, k + 1):
                u[m] = u[m] * r[m]
                x[m] = x[m] * r[m]
                if near is not None:
                    near[m] = near[m] * r[m]
                for i in range(m + 1, SUB):
                    u[i] = u[i] - l[m, i] * u[m]
                    x[i] = x[i] - l[m, i] * x[m]
                    if near is not None:
                        near[i] = near[i] - l[m, i] * near[m]
        final_u, final_x = u[0], x[0]
        for i in range(1, SUB):
            final_u = jnp.where(sub == i, u[i], final_u)
            final_x = jnp.where(sub == i, x[i], final_x)
        out_u.append(jnp.where(lane >= sub + base, final_u * unscale, 0.0))
        out_x.append(final_x * scale)
        if near is not None:
            nxt, nxt_x = rows[g + 1], eyes[g + 1]
            for k in range(SUB):
                nxt = nxt - near[k] * u[k]
                nxt_x = nxt_x - near[k] * x[k]
        if g + 2 < groups:
            v, vx = list(u), list(x)
            for i in reversed(range(SUB)):
                for j in range(i + 1, SUB):
                    v[i] = v[i] - l[i, j] * v[j]
                    vx[i] = vx[i] - l[i, j] * vx[j]
                v[i] = v[i] * r[i]
                vx[i] = vx[i] * r[i]
            for h in range(g + 2, groups):
                far, far_x = rows[h], eyes[h]
                for j in range(SUB):
                    c = spread(rows[h][:, base + j : base + j + 1])
                    far = far - c * v[j]
                    far_x = far_x - c * vx[j]
                rows[h], eyes[h] = far, far_x
        if near is not None:
            rows[g + 1], eyes[g + 1] = nxt, nxt_x
    return jnp.concatenate(out_u, axis=0), jnp.concatenate(out_x, axis=0)


def finish_blocks(u11, u12, x11, rest, u_ref, x_ref):
    zero = jnp.zeros((HALF, HALF), jnp.float32)
    u22, x22 = factor_half(rest)
    u_ref[:HALF, :HALF] = u11
    u_ref[:HALF, HALF:] = u12
    u_ref[HALF:, :HALF] = zero
    u_ref[HALF:, HALF:] = u22
    x_ref[:HALF, :HALF] = x11
    x_ref[:HALF, HALF:] = zero
    x_ref[HALF:, :HALF] = -mm(x22, t_mm(u12, x11))
    x_ref[HALF:, HALF:] = x22


def factor_blocks(s11, s12, s22, u_ref, x_ref):
    u11, x11 = factor_half(s11)
    u12 = mm(x11, s12)
    finish_blocks(u11, u12, x11, s22 - t_mm(u12, u12), u_ref, x_ref)


def tile_from(ref, start, stride):
    return jnp.concatenate(
        [ref[pl.ds(start, NB, stride=stride), :], ref[pl.ds(start + 1, NB, stride=stride), :]], axis=1
    )


def pack_kernel(loc_rows, loc_cols, own, top_a, top_b, *left):
    stride = 2 * loc_cols
    for a in range(loc_rows):
        left[a][...] = tile_from(own, a * NB * stride, stride)
    half = HALF * stride
    top_a[...] = own[:half, :]
    top_b[...] = own[half : 2 * half, :]


def first_kernel(pos, mine, other, u_ref, x_ref):
    s = jnp.where(pos[0] % 2 == 0, mine[...], other[...])
    factor_blocks(s[:HALF, :HALF], s[:HALF, HALF:], s[HALF:, HALF:], u_ref, x_ref)


def second_kernel(pos, x0, mine0, mine1, other0, other1, u_ref, x_ref, w_ref):
    even = pos[0] % 2 == 0
    u01 = mm(x0[...], jnp.where(even, mine1[...], other1[...]))
    s = jnp.where(even, other0[...], mine1[...]) - t_mm(u01, u01)
    factor_blocks(s[:HALF, :HALF], s[:HALF, HALF:], s[HALF:, HALF:], u_ref, x_ref)
    w_ref[...] = -mm(x_ref[...], t_mm(u01, x0[...]))


def last_kernel(
    loc_rows, loc_cols, pos, own, mine_a, mine_b, other_a, other_b, u0, x0, u1, x1, w, *rest
):
    left, right = rest[:loc_rows], rest[loc_rows : 2 * loc_rows]
    out, prows = rest[2 * loc_rows :]
    stride = 2 * loc_cols
    even = pos[0] % 2 == 0
    even_col = pos[1] % 2 == 0
    for a in range(loc_rows):
        l, r = left[a][...], right[a][...]
        b0, b1 = jnp.where(even_col, l, r), jnp.where(even_col, r, l)
        prows[2 * a] = mm_t(b0, x0[...], HIGH)
        prows[2 * a + 1] = mm_t(b0, w[...], HIGH) + mm_t(b1, x1[...], HIGH)

    def top_tile(a, b, start):
        halves = [
            jnp.concatenate(
                [ref[pl.ds(start + k, HALF, stride=stride), :] for k in (0, 1)], axis=1
            )
            for ref in (a, b)
        ]
        return jnp.concatenate(halves, axis=0)

    for b in range(loc_cols):
        tile_col = pos[1] + b * pos[3]
        e, o = top_tile(mine_a, mine_b, 2 * b), top_tile(other_a, other_b, 2 * b)
        d0, d1 = jnp.where(even, e, o), jnp.where(even, o, e)
        q0 = mm(x0[...], d0, HIGH)
        q1 = mm(w[...], d0, HIGH) + mm(x1[...], d1, HIGH)
        for a in range(loc_rows):
            tile_row = pos[0] + a * pos[2]
            start = a * NB * stride + 2 * b

            def put(value, start=start):
                out[pl.ds(start, NB, stride=stride), :] = value[:, :HALF]
                out[pl.ds(start + 1, NB, stride=stride), :] = value[:, HALF:]

            @pl.when(tile_row < tile_col)
            def _():
                put(jnp.zeros((NB, NB), jnp.float32))

            @pl.when((tile_row >= tile_col) & (tile_col >= 2))
            def _():
                put(
                    tile_from(own, start, stride)
                    - (mm(prows[2 * a], q0, HIGH) + mm(prows[2 * a + 1], q1, HIGH))
                )

            if b == 0:

                @pl.when((tile_row > 0) & (tile_col == 0))
                def _():
                    put(prows[2 * a])

                @pl.when((tile_row > 1) & (tile_col == 1))
                def _():
                    put(prows[2 * a + 1])

                if a == 0:

                    @pl.when((tile_row == 0) & (tile_col == 0))
                    def _():
                        put(u0[...].T)

                    @pl.when((tile_row == 1) & (tile_col == 1))
                    def _():
                        put(u1[...].T)


VMEM = pl.BlockSpec(memory_space=pltpu.VMEM)
SMEM = pl.BlockSpec(memory_space=pltpu.SMEM)


def shape(*dims):
    return jax.ShapeDtypeStruct(dims, jnp.float32)


def call(kernel, out_shape, flops, *args, smem=0, vmem=16, scratch=()):
    return pl.pallas_call(
        kernel,
        out_shape=out_shape,
        in_specs=[SMEM] * smem + [VMEM] * (len(args) - smem),
        out_specs=jax.tree.map(lambda _: VMEM, out_shape),
        scratch_shapes=list(scratch),
        compiler_params=pltpu.CompilerParams(vmem_limit_bytes=vmem * 2**20),
        cost_estimate=pl.CostEstimate(flops=flops, bytes_accessed=2**22, transcendentals=0),
    )(*args)


def on_device(n_row, n_col, trailing_in):
    row = lax.axis_index("row")
    col = lax.axis_index("col")
    loc_rows, _, _, loc_cols, _, _ = trailing_in.shape
    stride = 2 * loc_cols
    chips = n_row // 2
    chip = row // 2
    own = trailing_in.reshape(loc_rows * NB * stride, HALF)
    pos = jnp.stack([row, col, jnp.int32(n_row), jnp.int32(n_col)]).astype(jnp.int32)
    row_bits = [1 << k for k in range(1, (n_row - 1).bit_length())]
    col_bits = [1 << k for k in range(1, (n_col - 1).bit_length())][::-1]
    after = lax.optimization_barrier

    def swap(value, axis, bits):
        size = n_row if axis == "row" else n_col
        return lax.ppermute(value, axis, [(i, i ^ bits) for i in range(size)])

    def pick(index, values):
        out = values[0]
        for k, value in enumerate(values[1:], 1):
            out = jnp.where(index == k, value, out)
        return out

    def settle(value, axis, bit, got):
        return jnp.where((row if axis == "row" else col) & bit != 0, got, value)

    half = HALF * stride
    top_a, top_b, *left = call(
        functools.partial(pack_kernel, loc_rows, loc_cols),
        [shape(half, HALF), shape(half, HALF)] + [shape(NB, NB)] * loc_rows,
        10**8,
        own,
    )

    size = NB // chips
    pieces = [left[0][k * size : (k + 1) * size] for k in range(chips)]
    got = [swap(pieces[k], "row", 2 * k) for k in range(1, chips)]
    top_a, top_b, got = after((top_a, top_b, got))
    got_a, got_b = swap(top_a, "row", row_bits[0]), swap(top_b, "row", row_bits[-1])
    piece = pick(chip, [pieces[0]] + got)
    along = [piece] + [swap(piece, "col", k) for k in range(1, n_col)]
    got_a, got_b, along = after((got_a, got_b, along))
    pair = jnp.concatenate([pick(col, along), pick(col ^ 1, along)], axis=0)
    left, pair = after((left, pair))
    got_left = [swap(value, "col", col_bits[0]) for value in left]
    got = [pair] + [swap(pair, "row", 2 * k) for k in range(1, chips)]
    lead = [
        jnp.concatenate(
            [pick(chip ^ k, got)[j * size : (j + 1) * size] for k in range(chips)], axis=0
        )
        for j in (0, 1)
    ]
    lead_other = swap(jnp.where(row % 2 == 0, lead[0], lead[1]), "row", 1)

    def columns(a):
        value = settle(left[a], "col", col_bits[0], got_left[a])
        for bit in col_bits[1:]:
            value = settle(value, "col", bit, swap(value, "col", bit))
        return value, swap(value, "col", 1)

    top_a, top_b, lead[0] = after((top_a, top_b, lead[0]))
    top_a = settle(top_a, "row", row_bits[0], got_a)
    top_b = settle(top_b, "row", row_bits[-1], got_b)
    for first, second in zip(row_bits[1:-1], row_bits[-2:0:-1]):
        top_a = settle(top_a, "row", first, swap(top_a, "row", first))
        top_b = settle(top_b, "row", second, swap(top_b, "row", second))
    got_a, got_b = swap(top_a, "row", row_bits[-1]), swap(top_b, "row", row_bits[0])
    u0, x0 = call(first_kernel, [shape(NB, NB)] * 2, 10**10, pos, lead[0], lead_other, smem=1)

    got_a, got_b, got_left, lead[1], x0 = after((got_a, got_b, got_left, lead[1], x0))
    lead_next = swap(lead[1], "row", 1)
    both = [columns(a) for a in range(loc_rows)]
    left, right = [b[0] for b in both], [b[1] for b in both]
    top_a = settle(top_a, "row", row_bits[-1], got_a)
    top_b = settle(top_b, "row", row_bits[0], got_b)
    other_a, other_b = swap(top_a, "row", 1), swap(top_b, "row", 1)
    u1, x1, w = call(
        second_kernel,
        [shape(NB, NB)] * 3,
        10**10,
        pos, x0, lead[0], lead[1], lead_other, lead_next,
        smem=1,
    )
    right, other_a, other_b, x1 = after((right, other_a, other_b, x1))
    out = call(
        functools.partial(last_kernel, loc_rows, loc_cols),
        shape(*own.shape),
        10**7,
        pos, own, top_a, top_b, other_a, other_b, u0, x0, u1, x1, w, *left, *right,
        smem=1,
        vmem=24,
        scratch=[pltpu.VMEM((2 * loc_rows, NB, NB), jnp.float32)],
    )
    return out.reshape(trailing_in.shape)


def solution(mesh):
    return jax.shard_map(
        functools.partial(on_device, mesh.shape["row"], mesh.shape["col"]),
        mesh=mesh,
        in_specs=(P(None, "row", None, None, "col", None),),
        out_specs=P(None, "row", None, None, "col", None),
        check_vma=False,
    )
```

profile of v0, /device:TPU:0, one launch (start us, length us, event | category | flops | bytes accessed | tf_op | source)
XLA Modules:
  0.0 71.0 jit_solution(10687666007772211683)
XLA Ops:
  0.0 1.6 %copy-done = f32[2,1,256,4,1,256]{5,4,3,2,1,0:T(1,128)S(1)} copy-done((f32[2,1,256,4,1,256]{5,4,3,2,1,0:T(1,128)S(1)}, f32[2,1,256,4,1,256]{5,4,3,2,1,0:T(1,128)}, u32[]{:S(2)}) %copy-start) | copy-done | bytes 2097176
  1.6 0.2 shard_map.17
  1.8 4.0 %collective-permute-start.2 = (f32[64,256]{1,0:T(8,128)S(1)}, f32[64,256]{1,0:T(8,128)S(1)}, u32[]{:S(2)}, u32[]{:S(2)}) collective-permute-start(f32[64,256]{1,0:T(8,128)S(1)} %get-tuple-element.88), channel_id=1, source_target_pairs={{0,24},{4,28},{8,16},{12,20},{16,8},{20,12},{24,0},{28,4},{1,25},{... | collective-permute-start | bytes 196616 | tf_op jit(solution)/shard_map/ppermute | solution.py:275
  5.7 0.5 collective-permute-start.1
  6.4 1.6 %collective-permute-done.2 = f32[64,256]{1,0:T(8,128)S(1)} collective-permute-done((f32[64,256]{1,0:T(8,128)S(1)}, f32[64,256]{1,0:T(8,128)S(1)}, u32[]{:S(2)}, u32[]{:S(2)}) %collective-permute-start.2) | collective-permute-done | bytes 65568 | tf_op jit(solution)/shard_map/ppermute | solution.py:275
  8.0 2.0 %collective-permute-done.1 = f32[64,256]{1,0:T(8,128)S(1)} collective-permute-done((f32[64,256]{1,0:T(8,128)S(1)}, f32[64,256]{1,0:T(8,128)S(1)}, u32[]{:S(2)}, u32[]{:S(2)}) %collective-permute-start.1) | collective-permute-done | bytes 65568 | tf_op jit(solution)/shard_map/ppermute | solution.py:275
  10.0 0.5 collective-permute-done
  10.5 0.5 collective-permute-start.3
  11.0 1.6 %collective-permute-start.4 = (f32[1024,128]{1,0:T(8,128)S(1)}, f32[1024,128]{1,0:T(8,128)S(1)}, u32[]{:S(2)}, u32[]{:S(2)}) collective-permute-start(f32[1024,128]{1,0:T(8,128)S(1)} %get-tuple-element.59), channel_id=1, source_target_pairs={{0,16},{4,20},{8,24},{12,28},{16,0},{20,4},{24,8},{28,12},{1,17},{... | collective-permute-start | bytes 1572872 | tf_op jit(solution)/shard_map/ppermute | solution.py:275
  12.6 3.7 %collective-permute-start.7 = (f32[64,256]{1,0:T(8,128)S(1)}, f32[64,256]{1,0:T(8,128)S(1)}, u32[]{:S(2)}, u32[]{:S(2)}) collective-permute-start(f32[64,256]{1,0:T(8,128)S(1)} %select_select_fusion.6), channel_id=1, source_target_pairs={{0,3},{1,2},{2,1},{3,0},{4,7},{5,6},{6,5},{7,4},{8,11},{9,10},{10,... | collective-permute-start | bytes 196616 | tf_op jit(solution)/shard_map/ppermute | solution.py:275
  16.3 0.8 %collective-permute-start.5 = (f32[64,256]{1,0:T(8,128)S(1)}, f32[64,256]{1,0:T(8,128)S(1)}, u32[]{:S(2)}, u32[]{:S(2)}) collective-permute-start(f32[64,256]{1,0:T(8,128)S(1)} %select_select_fusion.6), channel_id=1, source_target_pairs={{0,1},{1,0},{2,3},{3,2},{4,5},{5,4},{6,7},{7,6},{8,9},{9,8},{10,11... | collective-permute-start | bytes 196616 | tf_op jit(solution)/shard_map/ppermute | solution.py:275
  17.0 1.8 %collective-permute-done.7 = f32[64,256]{1,0:T(8,128)S(1)} collective-permute-done((f32[64,256]{1,0:T(8,128)S(1)}, f32[64,256]{1,0:T(8,128)S(1)}, u32[]{:S(2)}, u32[]{:S(2)}) %collective-permute-start.7) | collective-permute-done | bytes 65568 | tf_op jit(solution)/shard_map/ppermute | solution.py:275
  18.8 2.6 %collective-permute-done.6 = f32[64,256]{1,0:T(8,128)S(1)} collective-permute-done((f32[64,256]{1,0:T(8,128)S(1)}, f32[64,256]{1,0:T(8,128)S(1)}, u32[]{:S(2)}, u32[]{:S(2)}) %collective-permute-start.6) | collective-permute-done | bytes 65568 | tf_op jit(solution)/shard_map/ppermute | solution.py:275
  21.4 1.4 %collective-permute-done.3 = f32[1024,128]{1,0:T(8,128)S(1)} collective-permute-done((f32[1024,128]{1,0:T(8,128)S(1)}, f32[1024,128]{1,0:T(8,128)S(1)}, u32[]{:S(2)}, u32[]{:S(2)}) %collective-permute-start.3) | collective-permute-done | bytes 524320 | tf_op jit(solution)/shard_map/ppermute | solution.py:275
  22.9 0.9 %collective-permute-done.4 = f32[1024,128]{1,0:T(8,128)S(1)} collective-permute-done((f32[1024,128]{1,0:T(8,128)S(1)}, f32[1024,128]{1,0:T(8,128)S(1)}, u32[]{:S(2)}, u32[]{:S(2)}) %collective-permute-start.4) | collective-permute-done | bytes 524320 | tf_op jit(solution)/shard_map/ppermute | solution.py:275
  23.9 0.9 %collective-permute-start.10 = (f32[128,256]{1,0:T(8,128)S(1)}, f32[128,256]{1,0:T(8,128)S(1)}, u32[]{:S(2)}, u32[]{:S(2)}) collective-permute-start(f32[128,256]{1,0:T(8,128)S(1)} %pad_maximum_fusion.2), channel_id=1, source_target_pairs={{0,8},{4,12},{8,0},{12,4},{16,24},{20,28},{24,16},{28,20},{1,9},{5... | collective-permute-start | bytes 393224 | tf_op jit(solution)/shard_map/ppermute | solution.py:275
  24.7 1.4 %collective-permute-start.9 = (f32[128,256]{1,0:T(8,128)S(1)}, f32[128,256]{1,0:T(8,128)S(1)}, u32[]{:S(2)}, u32[]{:S(2)}) collective-permute-start(f32[128,256]{1,0:T(8,128)S(1)} %pad_maximum_fusion.2), channel_id=1, source_target_pairs={{0,16},{4,20},{8,24},{12,28},{16,0},{20,4},{24,8},{28,12},{1,17},{... | collective-permute-start | bytes 393224 | tf_op jit(solution)/shard_map/ppermute | solution.py:275
  26.1 1.3 %collective-permute-start.8 = (f32[128,256]{1,0:T(8,128)S(1)}, f32[128,256]{1,0:T(8,128)S(1)}, u32[]{:S(2)}, u32[]{:S(2)}) collective-permute-start(f32[128,256]{1,0:T(8,128)S(1)} %pad_maximum_fusion.2), channel_id=1, source_target_pairs={{0,24},{4,28},{8,16},{12,20},{16,8},{20,12},{24,0},{28,4},{1,25},{... | collective-permute-start | bytes 393224 | tf_op jit(solution)/shard_map/ppermute | solution.py:275
  27.5 2.6 %collective-permute-start.13 = (f32[256,256]{1,0:T(8,128)S(1)}, f32[256,256]{1,0:T(8,128)S(1)}, u32[]{:S(2)}, u32[]{:S(2)}) collective-permute-start(f32[256,256]{1,0:T(8,128)S(1)} %get-tuple-element.60), channel_id=1, source_target_pairs={{0,2},{1,3},{2,0},{3,1},{4,6},{5,7},{6,4},{7,5},{8,10},{9,11},{10,... | collective-permute-start | bytes 786440 | tf_op jit(solution)/shard_map/ppermute | solution.py:275
  30.1 0.3 collective-permute-start.14
  30.4 1.6 %collective-permute-done.8 = f32[128,256]{1,0:T(8,128)S(1)} collective-permute-done((f32[128,256]{1,0:T(8,128)S(1)}, f32[128,256]{1,0:T(8,128)S(1)}, u32[]{:S(2)}, u32[]{:S(2)}) %collective-permute-start.8) | collective-permute-done | bytes 131104 | tf_op jit(solution)/shard_map/ppermute | solution.py:275
  32.3 0.9 %collective-permute-start.12 = (f32[1024,128]{1,0:T(8,128)S(1)}, f32[1024,128]{1,0:T(8,128)S(1)}, u32[]{:S(2)}, u32[]{:S(2)}) collective-permute-start(f32[1024,128]{1,0:T(8,128)S(1)} %broadcast_select_fusion.3), channel_id=1, source_target_pairs={{0,8},{4,12},{8,0},{12,4},{16,24},{20,28},{24,16},{28,20},{1,9},{5... | collective-permute-start | bytes 1572872 | tf_op jit(solution)/shard_map/ppermute | solution.py:275
  33.3 1.0 %collective-permute-start.11 = (f32[1024,128]{1,0:T(8,128)S(1)}, f32[1024,128]{1,0:T(8,128)S(1)}, u32[]{:S(2)}, u32[]{:S(2)}) collective-permute-start(f32[1024,128]{1,0:T(8,128)S(1)} %broadcast_select_fusion.1), channel_id=1, source_target_pairs={{0,16},{4,20},{8,24},{12,28},{16,0},{20,4},{24,8},{28,12},{1,17},{... | collective-permute-start | bytes 1572872 | tf_op jit(solution)/shard_map/ppermute | solution.py:275
  34.4 8.4 %shard_map.18 = (f32[256,256]{1,0:T(8,128)S(1)}, f32[256,256]{1,0:T(8,128)S(1)}) custom-call(s32[4]{0:T(128)S(1)} %pad_add_fusion.pos, f32[256,256]{1,0:T(8,128)S(1)} %get-tuple-element.62.mine.mine0, f32[256,256]{1,0:T(8,128)S(1)} %collective-permute-done.15.other.other0), custom_call_target="tpu_custom_call" | custom-call | flops 10000000000 | bytes 4194304 | tf_op jit(solution)/shard_map/pallas_call | solution.py:249
  42.8 3.4 %collective-permute-done.13 = f32[256,256]{1,0:T(8,128)S(1)} collective-permute-done((f32[256,256]{1,0:T(8,128)S(1)}, f32[256,256]{1,0:T(8,128)S(1)}, u32[]{:S(2)}, u32[]{:S(2)}) %collective-permute-start.13) | collective-permute-done | bytes 262176 | tf_op jit(solution)/shard_map/ppermute | solution.py:275
  46.2 4.5 %collective-permute-done.14 = f32[256,256]{1,0:T(8,128)S(1)} collective-permute-done((f32[256,256]{1,0:T(8,128)S(1)}, f32[256,256]{1,0:T(8,128)S(1)}, u32[]{:S(2)}, u32[]{:S(2)}) %collective-permute-start.14) | collective-permute-done | bytes 262176 | tf_op jit(solution)/shard_map/ppermute | solution.py:275
  50.9 0.7 collective-permute-start.16
  51.5 1.4 %collective-permute-start.17 = (f32[256,256]{1,0:T(8,128)S(1)}, f32[256,256]{1,0:T(8,128)S(1)}, u32[]{:S(2)}, u32[]{:S(2)}) collective-permute-start(f32[256,256]{1,0:T(8,128)S(1)} %broadcast_select_fusion.4.rest_1_), channel_id=1, source_target_pairs={{0,1},{1,0},{2,3},{3,2},{4,5},{5,4},{6,7},{7,6},{8,9},{9,8},{10,11... | collective-permute-start | bytes 786440 | tf_op jit(solution)/shard_map/ppermute | solution.py:275
  53.0 0.5 collective-permute-start.19
  53.6 0.9 %collective-permute-done.20.other1 = f32[256,256]{1,0:T(8,128)S(1)} collective-permute-done((f32[256,256]{1,0:T(8,128)S(1)}, f32[256,256]{1,0:T(8,128)S(1)}, u32[]{:S(2)}, u32[]{:S(2)}) %collective-permute-start.20) | collective-permute-done | bytes 262176 | tf_op jit(solution)/shard_map/ppermute | solution.py:275
  54.5 10.2 %shard_map.19 = (f32[256,256]{1,0:T(8,128)S(1)}, f32[256,256]{1,0:T(8,128)S(1)}, f32[256,256]{1,0:T(8,128)S(1)}) custom-call(s32[4]{0:T(128)S(1)} %pad_add_fusion.pos, f32[256,256]{1,0:T(8,128)S(1)} %get-tuple-element.68.x0, f32[256,256]{1,0:T(8,128)S(1)} %get-tuple-element.62.mine.mine0, f32[256,256]{1,0:T(8,128)S(1)} %get-tuple-element.69.mine1, ...), custom_call_target="tpu_custom_call" | custom-call | flops 10000000000 | bytes 4194304 | tf_op jit(solution)/shard_map/pallas_call | solution.py:249
  64.8 6.2 %shard_map.20 = f32[4096,128]{1,0:T(8,128)} custom-call(s32[4]{0:T(128)S(1)} %pad_add_fusion.pos, f32[4096,128]{1,0:T(8,128)S(1)} %bitcast.5, f32[1024,128]{1,0:T(8,128)S(1)} %broadcast_select_fusion.2.mine_a, f32[1024,128]{1,0:T(8,128)S(1)} %broadcast_select_fusion.mine_b, f32[1024,128]{1,0:T(8,128)S(1)} %collective-permute-done.18.other_a, ...), custom_call_target="tpu_custom_call" | custom-call | flops 10000000 | bytes 4194304 | tf_op jit(solution)/shard_map/pallas_call | solution.py:249
  (33 shorter events, 0.9 us)
Async XLA Ops:
  0.0 1.6 %copy-start = (f32[2,1,256,4,1,256]{5,4,3,2,1,0:T(1,128)S(1)}, f32[2,1,256,4,1,256]{5,4,3,2,1,0:T(1,128)}, u32[]{:S(2)}) copy-start(f32[2,1,256,4,1,256]{5,4,3,2,1,0:T(1,128)} %param.1) | copy-start | bytes 6291460
  1.8 6.2 %collective-permute-start.2 = (f32[64,256]{1,0:T(8,128)S(1)}, f32[64,256]{1,0:T(8,128)S(1)}, u32[]{:S(2)}, u32[]{:S(2)}) collective-permute-start(f32[64,256]{1,0:T(8,128)S(1)} %get-tuple-element.88), channel_id=1, source_target_pairs={{0,24},{4,28},{8,16},{12,20},{16,8},{20,12},{24,0},{28,4},{1,25},{... | collective-permute-start | bytes 196616 | tf_op jit(solution)/shard_map/ppermute | solution.py:275
  5.7 4.3 %collective-permute-start.1 = (f32[64,256]{1,0:T(8,128)S(1)}, f32[64,256]{1,0:T(8,128)S(1)}, u32[]{:S(2)}, u32[]{:S(2)}) collective-permute-start(f32[64,256]{1,0:T(8,128)S(1)} %get-tuple-element.89), channel_id=1, source_target_pairs={{0,16},{4,20},{8,24},{12,28},{16,0},{20,4},{24,8},{28,12},{1,17},{... | collective-permute-start | bytes 196616 | tf_op jit(solution)/shard_map/ppermute | solution.py:275
  6.3 4.3 %collective-permute-start = (f32[64,256]{1,0:T(8,128)S(1)}, f32[64,256]{1,0:T(8,128)S(1)}, u32[]{:S(2)}, u32[]{:S(2)}) collective-permute-start(f32[64,256]{1,0:T(8,128)S(1)} %get-tuple-element.90), channel_id=1, source_target_pairs={{0,8},{4,12},{8,0},{12,4},{16,24},{20,28},{24,16},{28,20},{1,9},{5... | collective-permute-start | bytes 196616 | tf_op jit(solution)/shard_map/ppermute | solution.py:275
  10.5 12.4 %collective-permute-start.3 = (f32[1024,128]{1,0:T(8,128)S(1)}, f32[1024,128]{1,0:T(8,128)S(1)}, u32[]{:S(2)}, u32[]{:S(2)}) collective-permute-start(f32[1024,128]{1,0:T(8,128)S(1)} %get-tuple-element.57), channel_id=1, source_target_pairs={{0,8},{4,12},{8,0},{12,4},{16,24},{20,28},{24,16},{28,20},{1,9},{5... | collective-permute-start | bytes 1572872 | tf_op jit(solution)/shard_map/ppermute | solution.py:275
  11.0 12.8 %collective-permute-start.4 = (f32[1024,128]{1,0:T(8,128)S(1)}, f32[1024,128]{1,0:T(8,128)S(1)}, u32[]{:S(2)}, u32[]{:S(2)}) collective-permute-start(f32[1024,128]{1,0:T(8,128)S(1)} %get-tuple-element.59), channel_id=1, source_target_pairs={{0,16},{4,20},{8,24},{12,28},{16,0},{20,4},{24,8},{28,12},{1,17},{... | collective-permute-start | bytes 1572872 | tf_op jit(solution)/shard_map/ppermute | solution.py:275
  12.6 6.2 %collective-permute-start.7 = (f32[64,256]{1,0:T(8,128)S(1)}, f32[64,256]{1,0:T(8,128)S(1)}, u32[]{:S(2)}, u32[]{:S(2)}) collective-permute-start(f32[64,256]{1,0:T(8,128)S(1)} %select_select_fusion.6), channel_id=1, source_target_pairs={{0,3},{1,2},{2,1},{3,0},{4,7},{5,6},{6,5},{7,4},{8,11},{9,10},{10,... | collective-permute-start | bytes 196616 | tf_op jit(solution)/shard_map/ppermute | solution.py:275
  16.3 5.2 %collective-permute-start.6 = (f32[64,256]{1,0:T(8,128)S(1)}, f32[64,256]{1,0:T(8,128)S(1)}, u32[]{:S(2)}, u32[]{:S(2)}) collective-permute-start(f32[64,256]{1,0:T(8,128)S(1)} %select_select_fusion.6), channel_id=1, source_target_pairs={{0,2},{1,3},{2,0},{3,1},{4,6},{5,7},{6,4},{7,5},{8,10},{9,11},{10,... | collective-permute-start | bytes 196616 | tf_op jit(solution)/shard_map/ppermute | solution.py:275
  16.3 5.2 %collective-permute-start.5 = (f32[64,256]{1,0:T(8,128)S(1)}, f32[64,256]{1,0:T(8,128)S(1)}, u32[]{:S(2)}, u32[]{:S(2)}) collective-permute-start(f32[64,256]{1,0:T(8,128)S(1)} %select_select_fusion.6), channel_id=1, source_target_pairs={{0,1},{1,0},{2,3},{3,2},{4,5},{5,4},{6,7},{7,6},{8,9},{9,8},{10,11... | collective-permute-start | bytes 196616 | tf_op jit(solution)/shard_map/ppermute | solution.py:275
  23.9 6.6 %collective-permute-start.10 = (f32[128,256]{1,0:T(8,128)S(1)}, f32[128,256]{1,0:T(8,128)S(1)}, u32[]{:S(2)}, u32[]{:S(2)}) collective-permute-start(f32[128,256]{1,0:T(8,128)S(1)} %pad_maximum_fusion.2), channel_id=1, source_target_pairs={{0,8},{4,12},{8,0},{12,4},{16,24},{20,28},{24,16},{28,20},{1,9},{5... | collective-permute-start | bytes 393224 | tf_op jit(solution)/shard_map/ppermute | solution.py:275
  24.7 5.7 %collective-permute-start.9 = (f32[128,256]{1,0:T(8,128)S(1)}, f32[128,256]{1,0:T(8,128)S(1)}, u32[]{:S(2)}, u32[]{:S(2)}) collective-permute-start(f32[128,256]{1,0:T(8,128)S(1)} %pad_maximum_fusion.2), channel_id=1, source_target_pairs={{0,16},{4,20},{8,24},{12,28},{16,0},{20,4},{24,8},{28,12},{1,17},{... | collective-permute-start | bytes 393224 | tf_op jit(solution)/shard_map/ppermute | solution.py:275
  26.1 5.9 %collective-permute-start.8 = (f32[128,256]{1,0:T(8,128)S(1)}, f32[128,256]{1,0:T(8,128)S(1)}, u32[]{:S(2)}, u32[]{:S(2)}) collective-permute-start(f32[128,256]{1,0:T(8,128)S(1)} %pad_maximum_fusion.2), channel_id=1, source_target_pairs={{0,24},{4,28},{8,16},{12,20},{16,8},{20,12},{24,0},{28,4},{1,25},{... | collective-permute-start | bytes 393224 | tf_op jit(solution)/shard_map/ppermute | solution.py:275
  27.5 18.7 %collective-permute-start.13 = (f32[256,256]{1,0:T(8,128)S(1)}, f32[256,256]{1,0:T(8,128)S(1)}, u32[]{:S(2)}, u32[]{:S(2)}) collective-permute-start(f32[256,256]{1,0:T(8,128)S(1)} %get-tuple-element.60), channel_id=1, source_target_pairs={{0,2},{1,3},{2,0},{3,1},{4,6},{5,7},{6,4},{7,5},{8,10},{9,11},{10,... | collective-permute-start | bytes 786440 | tf_op jit(solution)/shard_map/ppermute | solution.py:275
  30.1 20.6 %collective-permute-start.14 = (f32[256,256]{1,0:T(8,128)S(1)}, f32[256,256]{1,0:T(8,128)S(1)}, u32[]{:S(2)}, u32[]{:S(2)}) collective-permute-start(f32[256,256]{1,0:T(8,128)S(1)} %get-tuple-element.61), channel_id=1, source_target_pairs={{0,2},{1,3},{2,0},{3,1},{4,6},{5,7},{6,4},{7,5},{8,10},{9,11},{10,... | collective-permute-start | bytes 786440 | tf_op jit(solution)/shard_map/ppermute | solution.py:275
  32.2 2.2 %collective-permute-start.15 = (f32[256,256]{1,0:T(8,128)S(1)}, f32[256,256]{1,0:T(8,128)S(1)}, u32[]{:S(2)}, u32[]{:S(2)}) collective-permute-start(f32[256,256]{1,0:T(8,128)S(1)} %get-tuple-element.83), channel_id=1, source_target_pairs={{0,4},{4,0},{8,12},{12,8},{16,20},{20,16},{24,28},{28,24},{1,5},{5... | collective-permute-start | bytes 786440 | tf_op jit(solution)/shard_map/ppermute | solution.py:275
  32.3 18.4 %collective-permute-start.12 = (f32[1024,128]{1,0:T(8,128)S(1)}, f32[1024,128]{1,0:T(8,128)S(1)}, u32[]{:S(2)}, u32[]{:S(2)}) collective-permute-start(f32[1024,128]{1,0:T(8,128)S(1)} %broadcast_select_fusion.3), channel_id=1, source_target_pairs={{0,8},{4,12},{8,0},{12,4},{16,24},{20,28},{24,16},{28,20},{1,9},{5... | collective-permute-start | bytes 1572872 | tf_op jit(solution)/shard_map/ppermute | solution.py:275
  33.3 17.4 %collective-permute-start.11 = (f32[1024,128]{1,0:T(8,128)S(1)}, f32[1024,128]{1,0:T(8,128)S(1)}, u32[]{:S(2)}, u32[]{:S(2)}) collective-permute-start(f32[1024,128]{1,0:T(8,128)S(1)} %broadcast_select_fusion.1), channel_id=1, source_target_pairs={{0,16},{4,20},{8,24},{12,28},{16,0},{20,4},{24,8},{28,12},{1,17},{... | collective-permute-start | bytes 1572872 | tf_op jit(solution)/shard_map/ppermute | solution.py:275
  50.9 13.9 %collective-permute-start.16 = (f32[256,256]{1,0:T(8,128)S(1)}, f32[256,256]{1,0:T(8,128)S(1)}, u32[]{:S(2)}, u32[]{:S(2)}) collective-permute-start(f32[256,256]{1,0:T(8,128)S(1)} %broadcast_select_fusion.5.rest_0_), channel_id=1, source_target_pairs={{0,1},{1,0},{2,3},{3,2},{4,5},{5,4},{6,7},{7,6},{8,9},{9,8},{10,11... | collective-permute-start | bytes 786440 | tf_op jit(solution)/shard_map/ppermute | solution.py:275
  51.5 13.2 %collective-permute-start.17 = (f32[256,256]{1,0:T(8,128)S(1)}, f32[256,256]{1,0:T(8,128)S(1)}, u32[]{:S(2)}, u32[]{:S(2)}) collective-permute-start(f32[256,256]{1,0:T(8,128)S(1)} %broadcast_select_fusion.4.rest_1_), channel_id=1, source_target_pairs={{0,1},{1,0},{2,3},{3,2},{4,5},{5,4},{6,7},{7,6},{8,9},{9,8},{10,11... | collective-permute-start | bytes 786440 | tf_op jit(solution)/shard_map/ppermute | solution.py:275
  53.0 1.5 %collective-permute-start.20 = (f32[256,256]{1,0:T(8,128)S(1)}, f32[256,256]{1,0:T(8,128)S(1)}, u32[]{:S(2)}, u32[]{:S(2)}) collective-permute-start(f32[256,256]{1,0:T(8,128)S(1)} %get-tuple-element.69.mine1), channel_id=1, source_target_pairs={{0,4},{4,0},{8,12},{12,8},{16,20},{20,16},{24,28},{28,24},{1,5},{5... | collective-permute-start | bytes 786440 | tf_op jit(solution)/shard_map/ppermute | solution.py:275
  53.0 11.8 %collective-permute-start.19 = (f32[1024,128]{1,0:T(8,128)S(1)}, f32[1024,128]{1,0:T(8,128)S(1)}, u32[]{:S(2)}, u32[]{:S(2)}) collective-permute-start(f32[1024,128]{1,0:T(8,128)S(1)} %broadcast_select_fusion.mine_b), channel_id=1, source_target_pairs={{0,4},{4,0},{8,12},{12,8},{16,20},{20,16},{24,28},{28,24},{1,5},{5... | collective-permute-start | bytes 1572872 | tf_op jit(solution)/shard_map/ppermute | solution.py:275
  53.5 11.3 %copy-start.1 = (f32[2,1,256,4,1,256]{5,4,3,2,1,0:T(1,128)S(1)}, f32[2,1,256,4,1,256]{5,4,3,2,1,0:T(1,128)}, u32[]{:S(2)}) copy-start(f32[2,1,256,4,1,256]{5,4,3,2,1,0:T(1,128)} %param.1) | copy-start | bytes 6291460
  53.5 11.2 %collective-permute-start.18 = (f32[1024,128]{1,0:T(8,128)S(1)}, f32[1024,128]{1,0:T(8,128)S(1)}, u32[]{:S(2)}, u32[]{:S(2)}) collective-permute-start(f32[1024,128]{1,0:T(8,128)S(1)} %broadcast_select_fusion.2.mine_a), channel_id=1, source_target_pairs={{0,4},{4,0},{8,12},{12,8},{16,20},{20,16},{24,28},{28,24},{1,5},{5... | collective-permute-start | bytes 1572872 | tf_op jit(solution)/shard_map/ppermute | solution.py:275
where the time goes:
time: 71.2 us; the launch traced here: 71 us
  Pallas kernels  25 us (35%)
  starting transfers between devices  22.3 us (31%)
  waiting for transfers between devices  21.3 us (30%)
  local copies, waits for them, and re-layouts  1.65 us (2%)
    pallas_call x4, Pallas kernels, call(): pl.pallas_call(kernel, out_shape=out_shape, in_specs=[SMEM] * smem + [VME...  25 us
    ppermute x21, starting transfers between devices, swap(): return lax.ppermute(value, axis, [(i, i ^ bits) for i in range(size)])  22.3 us
    ppermute x21, waiting for transfers between devices, swap(): return lax.ppermute(value, axis, [(i, i ^ bits) for i in range(size)])  21.3 us
    unnamed x4, local copies, waits for them, and re-layouts  1.6 us
  transfers between devices with their start and end apart: 21, of which 11 were waited for; matrix products, arithmetic and copies ran while one was open for 1% of the time, Pallas kernels for 26%

commit v1 on v0

--- a/solution.py
+++ b/solution.py
@@ -168,19 +168,60 @@
     w_ref[...] = -mm(x_ref[...], t_mm(u01, x0[...]))
 
 
-def last_kernel(
-    loc_rows, loc_cols, pos, own, mine_a, mine_b, other_a, other_b, u0, x0, u1, x1, w, *rest
+def store_row(a, loc_cols, pos, prow0, prow1, q0, q1, u0, u1, own, out):
+    stride = 2 * loc_cols
+    tile_row = pos[0] + a * pos[2]
+    for b in range(loc_cols):
+        tile_col = pos[1] + b * pos[3]
+
+        def put(value, start=2 * b):
+            out[pl.ds(start, NB, stride=stride), :] = value[:, :HALF]
+            out[pl.ds(start + 1, NB, stride=stride), :] = value[:, HALF:]
+
+        @pl.when(tile_row < tile_col)
+        def _():
+            put(jnp.zeros((NB, NB), jnp.float32))
+
+        @pl.when((tile_row >= tile_col) & (tile_col >= 2))
+        def _():
+            put(
+                tile_from(own, 2 * b, stride)
+                - (mm(prow0, q0[b][...], HIGH) + mm(prow1, q1[b][...], HIGH))
+            )
+
+        if b == 0:
+
+            @pl.when((tile_row > 0) & (tile_col == 0))
+            def _():
+                put(prow0)
+
+            @pl.when((tile_row > 1) & (tile_col == 1))
+            def _():
+                put(prow1)
+
+            if a == 0:
+
+                @pl.when((tile_row == 0) & (tile_col == 0))
+                def _():
+                    put(u0[...].T)
+
+                @pl.when((tile_row == 1) & (tile_col == 1))
+                def _():
+                    put(u1[...].T)
+
+
+def panel_row(pos, left, right, x0, x1, w):
+    even_col = pos[1] % 2 == 0
+    l, r = left[...], right[...]
+    b0, b1 = jnp.where(even_col, l, r), jnp.where(even_col, r, l)
+    return mm_t(b0, x0[...], HIGH), mm_t(b0, w[...], HIGH) + mm_t(b1, x1[...], HIGH)
+
+
+def columns_kernel(
+    loc_cols, pos, own, left, right, mine_a, mine_b, other_a, other_b, u0, x0, u1, x1, w, out, *q
 ):
-    left, right = rest[:loc_rows], rest[loc_rows : 2 * loc_rows]
-    out, prows = rest[2 * loc_rows :]
     stride = 2 * loc_cols
     even = pos[0] % 2 == 0
-    even_col = pos[1] % 2 == 0
-    for a in range(loc_rows):
-        l, r = left[a][...], right[a][...]
-        b0, b1 = jnp.where(even_col, l, r), jnp.where(even_col, r, l)
-        prows[2 * a] = mm_t(b0, x0[...], HIGH)
-        prows[2 * a + 1] = mm_t(b0, w[...], HIGH) + mm_t(b1, x1[...], HIGH)
 
     def top_tile(a, b, start):
         halves = [
@@ -191,50 +232,22 @@
         ]
         return jnp.concatenate(halves, axis=0)
 
+    q0, q1 = q[:loc_cols], q[loc_cols:]
     for b in range(loc_cols):
-        tile_col = pos[1] + b * pos[3]
         e, o = top_tile(mine_a, mine_b, 2 * b), top_tile(other_a, other_b, 2 * b)
         d0, d1 = jnp.where(even, e, o), jnp.where(even, o, e)
-        q0 = mm(x0[...], d0, HIGH)
-        q1 = mm(w[...], d0, HIGH) + mm(x1[...], d1, HIGH)
-        for a in range(loc_rows):
-            tile_row = pos[0] + a * pos[2]
-            start = a * NB * stride + 2 * b
-
-            def put(value, start=start):
-                out[pl.ds(start, NB, stride=stride), :] = value[:, :HALF]
-                out[pl.ds(start + 1, NB, stride=stride), :] = value[:, HALF:]
-
-            @pl.when(tile_row < tile_col)
-            def _():
-                put(jnp.zeros((NB, NB), jnp.float32))
-
-            @pl.when((tile_row >= tile_col) & (tile_col >= 2))
-            def _():
-                put(
-                    tile_from(own, start, stride)
-                    - (mm(prows[2 * a], q0, HIGH) + mm(prows[2 * a + 1], q1, HIGH))
-                )
-
-            if b == 0:
-
-                @pl.when((tile_row > 0) & (tile_col == 0))
-                def _():
-                    put(prows[2 * a])
-
-                @pl.when((tile_row > 1) & (tile_col == 1))
-                def _():
-                    put(prows[2 * a + 1])
-
-                if a == 0:
-
-                    @pl.when((tile_row == 0) & (tile_col == 0))
-                    def _():
-                        put(u0[...].T)
-
-                    @pl.when((tile_row == 1) & (tile_col == 1))
-                    def _():
-                        put(u1[...].T)
+        q0[b][...] = mm(x0[...], d0, HIGH)
+        q1[b][...] = mm(w[...], d0, HIGH) + mm(x1[...], d1, HIGH)
+    prow0, prow1 = panel_row(pos, left, right, x0, x1, w)
+    store_row(0, loc_cols, pos, prow0, prow1, q0, q1, u0, u1, own, out)
+
+
+def later_kernel(a, loc_cols, pos, own, left, right, x0, x1, w, *rest):
+    q, out = rest[: 2 * loc_cols], rest[-1]
+    prow0, prow1 = panel_row(pos, left, right, x0, x1, w)
+    store_row(
+        a, loc_cols, pos, prow0, prow1, q[:loc_cols], q[loc_cols:], None, None, own, out
+    )
 
 
 VMEM = pl.BlockSpec(memory_space=pltpu.VMEM)
@@ -245,13 +258,16 @@
     return jax.ShapeDtypeStruct(dims, jnp.float32)
 
 
-def call(kernel, out_shape, flops, *args, smem=0, vmem=16, scratch=()):
+def call(
+    kernel, out_shape, flops, *args, smem=0, vmem=16, specs=None, out_specs=None, aliases=None, grid=()
+):
     return pl.pallas_call(
         kernel,
+        grid=grid,
         out_shape=out_shape,
-        in_specs=[SMEM] * smem + [VMEM] * (len(args) - smem),
-        out_specs=jax.tree.map(lambda _: VMEM, out_shape),
-        scratch_shapes=list(scratch),
+        in_specs=specs or [SMEM] * smem + [VMEM] * (len(args) - smem),
+        out_specs=out_specs or jax.tree.map(lambda _: VMEM, out_shape),
+        input_output_aliases=aliases or {},
         compiler_params=pltpu.CompilerParams(vmem_limit_bytes=vmem * 2**20),
         cost_estimate=pl.CostEstimate(flops=flops, bytes_accessed=2**22, transcendentals=0),
     )(*args)
@@ -300,8 +316,8 @@
     along = [piece] + [swap(piece, "col", k) for k in range(1, n_col)]
     got_a, got_b, along = after((got_a, got_b, along))
     pair = jnp.concatenate([pick(col, along), pick(col ^ 1, along)], axis=0)
-    left, pair = after((left, pair))
-    got_left = [swap(value, "col", col_bits[0]) for value in left]
+    left[0], pair = after((left[0], pair))
+    got_left = [swap(left[0], "col", col_bits[0])]
     got = [pair] + [swap(pair, "row", 2 * k) for k in range(1, chips)]
     lead = [
         jnp.concatenate(
@@ -326,13 +342,10 @@
     got_a, got_b = swap(top_a, "row", row_bits[-1]), swap(top_b, "row", row_bits[0])
     u0, x0 = call(first_kernel, [shape(NB, NB)] * 2, 10**10, pos, lead[0], lead_other, smem=1)
 
-    got_a, got_b, got_left, lead[1], x0 = after((got_a, got_b, got_left, lead[1], x0))
+    got_left, left[1:], lead[1], x0 = after((got_left, left[1:], lead[1], x0))
     lead_next = swap(lead[1], "row", 1)
-    both = [columns(a) for a in range(loc_rows)]
-    left, right = [b[0] for b in both], [b[1] for b in both]
-    top_a = settle(top_a, "row", row_bits[-1], got_a)
-    top_b = settle(top_b, "row", row_bits[0], got_b)
-    other_a, other_b = swap(top_a, "row", 1), swap(top_b, "row", 1)
+    got_left += [swap(value, "col", col_bits[0]) for value in left[1:]]
+    both = [columns(0)]
     u1, x1, w = call(
         second_kernel,
         [shape(NB, NB)] * 3,
@@ -340,16 +353,36 @@
         pos, x0, lead[0], lead[1], lead_other, lead_next,
         smem=1,
     )
-    right, other_a, other_b, x1 = after((right, other_a, other_b, x1))
-    out = call(
-        functools.partial(last_kernel, loc_rows, loc_cols),
-        shape(*own.shape),
-        10**7,
-        pos, own, top_a, top_b, other_a, other_b, u0, x0, u1, x1, w, *left, *right,
-        smem=1,
+    got_a, got_b, got_left[1:], both[0], x1 = after((got_a, got_b, got_left[1:], both[0], x1))
+    top_a = settle(top_a, "row", row_bits[-1], got_a)
+    top_b = settle(top_b, "row", row_bits[0], got_b)
+    other_a, other_b = swap(top_a, "row", 1), swap(top_b, "row", 1)
+    both += [columns(a) for a in range(1, loc_rows)]
+
+    def block(a):
+        return pl.BlockSpec((NB * stride, HALF), lambda i: (a, 0))
+
+    out, *q = call(
+        functools.partial(columns_kernel, loc_cols),
+        [shape(*own.shape)] + [shape(NB, NB)] * (2 * loc_cols),
+        10**9,
+        pos, own, *both[0], top_a, top_b, other_a, other_b, u0, x0, u1, x1, w,
+        specs=[SMEM, block(0)] + [VMEM] * 11,
+        out_specs=[block(0)] + [VMEM] * (2 * loc_cols),
+        grid=(1,),
         vmem=24,
-        scratch=[pltpu.VMEM((2 * loc_rows, NB, NB), jnp.float32)],
-    )
+    )
+    for a in range(1, loc_rows):
+        out = call(
+            functools.partial(later_kernel, a, loc_cols),
+            shape(*own.shape),
+            10**7,
+            pos, own, *both[a], x0, x1, w, *q, out,
+            specs=[SMEM, block(a)] + [VMEM] * (5 + 2 * loc_cols) + [pl.BlockSpec(memory_space=pl.ANY)],
+            out_specs=block(a),
+            aliases={7 + 2 * loc_cols: 0},
+            grid=(1,),
+        )
     return out.reshape(trailing_in.shape)
 
 

time: 71.2 us -> 71.6 us (level)
  waiting for transfers between devices: 21.3 us -> 18.8 us
  starting transfers between devices: 22.3 us -> 24.5 us
  Pallas kernels: 25 us -> 25.8 us
    ppermute x21, waiting for transfers between devices: 21.3 us -> 18.8 us  [swap(): return lax.ppermute(value, axis, [(i, i ^ bits) for i in range(size)])]
    ppermute x21, starting transfers between devices: 22.3 us -> 24.5 us  [swap(): return lax.ppermute(value, axis, [(i, i ^ bits) for i in range(size)])]
    pallas_call x4 -> x5, Pallas kernels: 25 us -> 25.8 us  [call(): pl.pallas_call(kernel, grid=grid, out_shape=out_shape, in_specs=specs or...]
  transfers between devices with their start and end apart: 21 -> 21, of which waited for: 11 -> 13; matrix products, arithmetic and copies ran while one was open for 1% -> 1% of each run, Pallas kernels for 26% -> 32%
where the time goes in v1:
time: 71.6 us; the launch traced here: 71.5 us
  Pallas kernels  25.8 us (36%)
  starting transfers between devices  24.5 us (34%)
  waiting for transfers between devices  18.8 us (26%)
  local copies, waits for them, and re-layouts  1.65 us (2%)
    pallas_call x5, Pallas kernels, call(): pl.pallas_call(kernel, grid=grid, out_shape=out_shape, in_specs=specs or...  25.8 us
    ppermute x21, starting transfers between devices, swap(): return lax.ppermute(value, axis, [(i, i ^ bits) for i in range(size)])  24.5 us
    ppermute x21, waiting for transfers between devices, swap(): return lax.ppermute(value, axis, [(i, i ^ bits) for i in range(size)])  18.8 us
    unnamed x4, local copies, waits for them, and re-layouts  1.6 us
  transfers between devices with their start and end apart: 21, of which 13 were waited for; matrix products, arithmetic and copies ran while one was open for 1% of the time, Pallas kernels for 32%

profile of v1, /device:TPU:0, one launch (start us, length us, event | category | flops | bytes accessed | tf_op | source)
XLA Modules:
  0.0 71.5 jit_solution(1262394956045656939)
XLA Ops:
  0.0 1.6 %copy-done = f32[2,1,256,4,1,256]{5,4,3,2,1,0:T(1,128)S(1)} copy-done((f32[2,1,256,4,1,256]{5,4,3,2,1,0:T(1,128)S(1)}, f32[2,1,256,4,1,256]{5,4,3,2,1,0:T(1,128)}, u32[]{:S(2)}) %copy-start) | copy-done | bytes 2097176
  1.8 4.0 %collective-permute-start.2 = (f32[64,256]{1,0:T(8,128)S(1)}, f32[64,256]{1,0:T(8,128)S(1)}, u32[]{:S(2)}, u32[]{:S(2)}) collective-permute-start(f32[64,256]{1,0:T(8,128)S(1)} %get-tuple-element.102), channel_id=1, source_target_pairs={{0,24},{4,28},{8,16},{12,20},{16,8},{20,12},{24,0},{28,4},{1,25},{... | collective-permute-start | bytes 196616 | tf_op jit(solution)/shard_map/ppermute | solution.py:291
  5.7 0.5 collective-permute-start.1
  6.4 1.6 %collective-permute-done.2 = f32[64,256]{1,0:T(8,128)S(1)} collective-permute-done((f32[64,256]{1,0:T(8,128)S(1)}, f32[64,256]{1,0:T(8,128)S(1)}, u32[]{:S(2)}, u32[]{:S(2)}) %collective-permute-start.2) | collective-permute-done | bytes 65568 | tf_op jit(solution)/shard_map/ppermute | solution.py:291
  8.0 2.0 %collective-permute-done.1 = f32[64,256]{1,0:T(8,128)S(1)} collective-permute-done((f32[64,256]{1,0:T(8,128)S(1)}, f32[64,256]{1,0:T(8,128)S(1)}, u32[]{:S(2)}, u32[]{:S(2)}) %collective-permute-start.1) | collective-permute-done | bytes 65568 | tf_op jit(solution)/shard_map/ppermute | solution.py:291
  10.0 0.5 collective-permute-done
  11.0 1.6 %collective-permute-start.4 = (f32[1024,128]{1,0:T(8,128)S(1)}, f32[1024,128]{1,0:T(8,128)S(1)}, u32[]{:S(2)}, u32[]{:S(2)}) collective-permute-start(f32[1024,128]{1,0:T(8,128)S(1)} %get-tuple-element.65), channel_id=1, source_target_pairs={{0,16},{4,20},{8,24},{12,28},{16,0},{20,4},{24,8},{28,12},{1,17},{... | collective-permute-start | bytes 1572872 | tf_op jit(solution)/shard_map/ppermute | solution.py:291
  12.6 3.7 %collective-permute-start.7 = (f32[64,256]{1,0:T(8,128)S(1)}, f32[64,256]{1,0:T(8,128)S(1)}, u32[]{:S(2)}, u32[]{:S(2)}) collective-permute-start(f32[64,256]{1,0:T(8,128)S(1)} %select_select_fusion.6), channel_id=1, source_target_pairs={{0,3},{1,2},{2,1},{3,0},{4,7},{5,6},{6,5},{7,4},{8,11},{9,10},{10,... | collective-permute-start | bytes 196616 | tf_op jit(solution)/shard_map/ppermute | solution.py:291
  16.3 0.8 %collective-permute-start.5 = (f32[64,256]{1,0:T(8,128)S(1)}, f32[64,256]{1,0:T(8,128)S(1)}, u32[]{:S(2)}, u32[]{:S(2)}) collective-permute-start(f32[64,256]{1,0:T(8,128)S(1)} %select_select_fusion.6), channel_id=1, source_target_pairs={{0,1},{1,0},{2,3},{3,2},{4,5},{5,4},{6,7},{7,6},{8,9},{9,8},{10,11... | collective-permute-start | bytes 196616 | tf_op jit(solution)/shard_map/ppermute | solution.py:291
  17.0 1.8 %collective-permute-done.7 = f32[64,256]{1,0:T(8,128)S(1)} collective-permute-done((f32[64,256]{1,0:T(8,128)S(1)}, f32[64,256]{1,0:T(8,128)S(1)}, u32[]{:S(2)}, u32[]{:S(2)}) %collective-permute-start.7) | collective-permute-done | bytes 65568 | tf_op jit(solution)/shard_map/ppermute | solution.py:291
  18.8 2.6 %collective-permute-done.6 = f32[64,256]{1,0:T(8,128)S(1)} collective-permute-done((f32[64,256]{1,0:T(8,128)S(1)}, f32[64,256]{1,0:T(8,128)S(1)}, u32[]{:S(2)}, u32[]{:S(2)}) %collective-permute-start.6) | collective-permute-done | bytes 65568 | tf_op jit(solution)/shard_map/ppermute | solution.py:291
  21.4 1.4 %collective-permute-done.3 = f32[1024,128]{1,0:T(8,128)S(1)} collective-permute-done((f32[1024,128]{1,0:T(8,128)S(1)}, f32[1024,128]{1,0:T(8,128)S(1)}, u32[]{:S(2)}, u32[]{:S(2)}) %collective-permute-start.3) | collective-permute-done | bytes 524320 | tf_op jit(solution)/shard_map/ppermute | solution.py:291
  22.9 0.9 %collective-permute-done.4 = f32[1024,128]{1,0:T(8,128)S(1)} collective-permute-done((f32[1024,128]{1,0:T(8,128)S(1)}, f32[1024,128]{1,0:T(8,128)S(1)}, u32[]{:S(2)}, u32[]{:S(2)}) %collective-permute-start.4) | collective-permute-done | bytes 524320 | tf_op jit(solution)/shard_map/ppermute | solution.py:291
  23.9 0.9 %collective-permute-start.10 = (f32[128,256]{1,0:T(8,128)S(1)}, f32[128,256]{1,0:T(8,128)S(1)}, u32[]{:S(2)}, u32[]{:S(2)}) collective-permute-start(f32[128,256]{1,0:T(8,128)S(1)} %pad_maximum_fusion.2), channel_id=1, source_target_pairs={{0,8},{4,12},{8,0},{12,4},{16,24},{20,28},{24,16},{28,20},{1,9},{5... | collective-permute-start | bytes 393224 | tf_op jit(solution)/shard_map/ppermute | solution.py:291
  24.7 1.4 %collective-permute-start.9 = (f32[128,256]{1,0:T(8,128)S(1)}, f32[128,256]{1,0:T(8,128)S(1)}, u32[]{:S(2)}, u32[]{:S(2)}) collective-permute-start(f32[128,256]{1,0:T(8,128)S(1)} %pad_maximum_fusion.2), channel_id=1, source_target_pairs={{0,16},{4,20},{8,24},{12,28},{16,0},{20,4},{24,8},{28,12},{1,17},{... | collective-permute-start | bytes 393224 | tf_op jit(solution)/shard_map/ppermute | solution.py:291
  26.1 1.3 %collective-permute-start.8 = (f32[128,256]{1,0:T(8,128)S(1)}, f32[128,256]{1,0:T(8,128)S(1)}, u32[]{:S(2)}, u32[]{:S(2)}) collective-permute-start(f32[128,256]{1,0:T(8,128)S(1)} %pad_maximum_fusion.2), channel_id=1, source_target_pairs={{0,24},{4,28},{8,16},{12,20},{16,8},{20,12},{24,0},{28,4},{1,25},{... | collective-permute-start | bytes 393224 | tf_op jit(solution)/shard_map/ppermute | solution.py:291
  27.5 2.6 %collective-permute-start.13 = (f32[256,256]{1,0:T(8,128)S(1)}, f32[256,256]{1,0:T(8,128)S(1)}, u32[]{:S(2)}, u32[]{:S(2)}) collective-permute-start(f32[256,256]{1,0:T(8,128)S(1)} %get-tuple-element.66), channel_id=1, source_target_pairs={{0,2},{1,3},{2,0},{3,1},{4,6},{5,7},{6,4},{7,5},{8,10},{9,11},{10,... | collective-permute-start | bytes 786440 | tf_op jit(solution)/shard_map/ppermute | solution.py:291
  30.1 1.9 %collective-permute-done.8 = f32[128,256]{1,0:T(8,128)S(1)} collective-permute-done((f32[128,256]{1,0:T(8,128)S(1)}, f32[128,256]{1,0:T(8,128)S(1)}, u32[]{:S(2)}, u32[]{:S(2)}) %collective-permute-start.8) | collective-permute-done | bytes 131104 | tf_op jit(solution)/shard_map/ppermute | solution.py:291
  32.3 0.9 %collective-permute-start.12 = (f32[1024,128]{1,0:T(8,128)S(1)}, f32[1024,128]{1,0:T(8,128)S(1)}, u32[]{:S(2)}, u32[]{:S(2)}) collective-permute-start(f32[1024,128]{1,0:T(8,128)S(1)} %broadcast_select_fusion.1), channel_id=1, source_target_pairs={{0,8},{4,12},{8,0},{12,4},{16,24},{20,28},{24,16},{28,20},{1,9},{5... | collective-permute-start | bytes 1572872 | tf_op jit(solution)/shard_map/ppermute | solution.py:291
  33.3 0.5 collective-permute-done.14.other.other0
  33.8 8.4 %shard_map.18 = (f32[256,256]{1,0:T(8,128)S(1)}, f32[256,256]{1,0:T(8,128)S(1)}) custom-call(s32[4]{0:T(128)S(1)} %pad_add_fusion.pos, f32[256,256]{1,0:T(8,128)S(1)} %get-tuple-element.68.mine.mine0, f32[256,256]{1,0:T(8,128)S(1)} %collective-permute-done.14.other.other0), custom_call_target="tpu_custom_call" | custom-call | flops 10000000000 | bytes 4194304 | tf_op jit(solution)/shard_map/pallas_call | solution.py:264
  42.5 0.7 collective-permute-start.11
  43.2 1.6 %collective-permute-start.16 = (f32[256,256]{1,0:T(8,128)S(1)}, f32[256,256]{1,0:T(8,128)S(1)}, u32[]{:S(2)}, u32[]{:S(2)}) collective-permute-start(f32[256,256]{1,0:T(8,128)S(1)} %broadcast_select_fusion.6.left), channel_id=1, source_target_pairs={{0,1},{1,0},{2,3},{3,2},{4,5},{5,4},{6,7},{7,6},{8,9},{9,8},{10,11... | collective-permute-start | bytes 786440 | tf_op jit(solution)/shard_map/ppermute | solution.py:291
  44.8 2.6 %collective-permute-start.15 = (f32[256,256]{1,0:T(8,128)S(1)}, f32[256,256]{1,0:T(8,128)S(1)}, u32[]{:S(2)}, u32[]{:S(2)}) collective-permute-start(f32[256,256]{1,0:T(8,128)S(1)} %get-tuple-element.70), channel_id=1, source_target_pairs={{0,2},{1,3},{2,0},{3,1},{4,6},{5,7},{6,4},{7,5},{8,10},{9,11},{10,... | collective-permute-start | bytes 786440 | tf_op jit(solution)/shard_map/ppermute | solution.py:291
  47.4 10.2 %shard_map.19 = (f32[256,256]{1,0:T(8,128)S(1)}, f32[256,256]{1,0:T(8,128)S(1)}, f32[256,256]{1,0:T(8,128)S(1)}) custom-call(s32[4]{0:T(128)S(1)} %pad_add_fusion.pos, f32[256,256]{1,0:T(8,128)S(1)} %get-tuple-element.72.x0, f32[256,256]{1,0:T(8,128)S(1)} %get-tuple-element.68.mine.mine0, f32[256,256]{1,0:T(8,128)S(1)} %get-tuple-element.73.mine1, ...), custom_call_target="tpu_custom_call" | custom-call | flops 10000000000 | bytes 4194304 | tf_op jit(solution)/shard_map/pallas_call | solution.py:264
  57.7 1.7 %collective-permute-done.15 = f32[256,256]{1,0:T(8,128)S(1)} collective-permute-done((f32[256,256]{1,0:T(8,128)S(1)}, f32[256,256]{1,0:T(8,128)S(1)}, u32[]{:S(2)}, u32[]{:S(2)}) %collective-permute-start.15) | collective-permute-done | bytes 262176 | tf_op jit(solution)/shard_map/ppermute | solution.py:291
  60.2 0.5 collective-permute-start.18
  60.7 0.8 %collective-permute-done.19.other_a = f32[1024,128]{1,0:T(8,128)S(1)} collective-permute-done((f32[1024,128]{1,0:T(8,128)S(1)}, f32[1024,128]{1,0:T(8,128)S(1)}, u32[]{:S(2)}, u32[]{:S(2)}) %collective-permute-start.19) | collective-permute-done | bytes 524320 | tf_op jit(solution)/shard_map/ppermute | solution.py:291
  61.5 0.7 %collective-permute-done.20.other_b = f32[1024,128]{1,0:T(8,128)S(1)} collective-permute-done((f32[1024,128]{1,0:T(8,128)S(1)}, f32[1024,128]{1,0:T(8,128)S(1)}, u32[]{:S(2)}, u32[]{:S(2)}) %collective-permute-start.20) | collective-permute-done | bytes 524320 | tf_op jit(solution)/shard_map/ppermute | solution.py:291
  62.3 4.1 %shard_map.20 = (f32[4096,128]{1,0:T(8,128)}, f32[256,256]{1,0:T(8,128)S(1)}, f32[256,256]{1,0:T(8,128)S(1)}, f32[256,256]{1,0:T(8,128)S(1)}, f32[256,256]{1,0:T...) custom-call(s32[4]{0:T(128)S(1)} %pad_add_fusion.pos, ...), custom_call_target="tpu_custom_call" | custom-call | flops 1000000000 | bytes 4194304 | tf_op jit(solution)/shard_map/pallas_call | solution.py:264
  66.3 2.2 %collective-permute-done.18.right = f32[256,256]{1,0:T(8,128)S(1)} collective-permute-done((f32[256,256]{1,0:T(8,128)S(1)}, f32[256,256]{1,0:T(8,128)S(1)}, u32[]{:S(2)}, u32[]{:S(2)}) %collective-permute-start.18) | collective-permute-done | bytes 262176 | tf_op jit(solution)/shard_map/ppermute | solution.py:291
  68.5 3.0 %shard_map.21 = f32[4096,128]{1,0:T(8,128)} custom-call(s32[4]{0:T(128)S(1)} %pad_add_fusion.pos, f32[4096,128]{1,0:T(8,128)S(1)} %bitcast.6, f32[256,256]{1,0:T(8,128)S(1)} %broadcast_select_fusion.5.left, f32[256,256]{1,0:T(8,128)S(1)} %collective-permute-done.18.right, f32[256,256]{1,0:T(8,128)S(1)} %get-tuple-element.72.x0, ...), custom_call_target="tpu_custom_call", output_to_operand_aliasing={{}: (15, {})} | custom-call | flops 10000000 | bytes 4194304 | tf_op jit(solution)/shard_map/pallas_call | solution.py:264
  (34 shorter events, 2.2 us)
Async XLA Ops:
  0.0 1.6 %copy-start = (f32[2,1,256,4,1,256]{5,4,3,2,1,0:T(1,128)S(1)}, f32[2,1,256,4,1,256]{5,4,3,2,1,0:T(1,128)}, u32[]{:S(2)}) copy-start(f32[2,1,256,4,1,256]{5,4,3,2,1,0:T(1,128)} %param.1) | copy-start | bytes 6291460
  1.8 6.2 %collective-permute-start.2 = (f32[64,256]{1,0:T(8,128)S(1)}, f32[64,256]{1,0:T(8,128)S(1)}, u32[]{:S(2)}, u32[]{:S(2)}) collective-permute-start(f32[64,256]{1,0:T(8,128)S(1)} %get-tuple-element.102), channel_id=1, source_target_pairs={{0,24},{4,28},{8,16},{12,20},{16,8},{20,12},{24,0},{28,4},{1,25},{... | collective-permute-start | bytes 196616 | tf_op jit(solution)/shard_map/ppermute | solution.py:291
  5.7 4.3 %collective-permute-start.1 = (f32[64,256]{1,0:T(8,128)S(1)}, f32[64,256]{1,0:T(8,128)S(1)}, u32[]{:S(2)}, u32[]{:S(2)}) collective-permute-start(f32[64,256]{1,0:T(8,128)S(1)} %get-tuple-element.103), channel_id=1, source_target_pairs={{0,16},{4,20},{8,24},{12,28},{16,0},{20,4},{24,8},{28,12},{1,17},{... | collective-permute-start | bytes 196616 | tf_op jit(solution)/shard_map/ppermute | solution.py:291
  6.3 4.3 %collective-permute-start = (f32[64,256]{1,0:T(8,128)S(1)}, f32[64,256]{1,0:T(8,128)S(1)}, u32[]{:S(2)}, u32[]{:S(2)}) collective-permute-start(f32[64,256]{1,0:T(8,128)S(1)} %get-tuple-element.104), channel_id=1, source_target_pairs={{0,8},{4,12},{8,0},{12,4},{16,24},{20,28},{24,16},{28,20},{1,9},{5... | collective-permute-start | bytes 196616 | tf_op jit(solution)/shard_map/ppermute | solution.py:291
  10.5 12.4 %collective-permute-start.3 = (f32[1024,128]{1,0:T(8,128)S(1)}, f32[1024,128]{1,0:T(8,128)S(1)}, u32[]{:S(2)}, u32[]{:S(2)}) collective-permute-start(f32[1024,128]{1,0:T(8,128)S(1)} %get-tuple-element.63), channel_id=1, source_target_pairs={{0,8},{4,12},{8,0},{12,4},{16,24},{20,28},{24,16},{28,20},{1,9},{5... | collective-permute-start | bytes 1572872 | tf_op jit(solution)/shard_map/ppermute | solution.py:291
  11.0 12.8 %collective-permute-start.4 = (f32[1024,128]{1,0:T(8,128)S(1)}, f32[1024,128]{1,0:T(8,128)S(1)}, u32[]{:S(2)}, u32[]{:S(2)}) collective-permute-start(f32[1024,128]{1,0:T(8,128)S(1)} %get-tuple-element.65), channel_id=1, source_target_pairs={{0,16},{4,20},{8,24},{12,28},{16,0},{20,4},{24,8},{28,12},{1,17},{... | collective-permute-start | bytes 1572872 | tf_op jit(solution)/shard_map/ppermute | solution.py:291
  12.6 6.2 %collective-permute-start.7 = (f32[64,256]{1,0:T(8,128)S(1)}, f32[64,256]{1,0:T(8,128)S(1)}, u32[]{:S(2)}, u32[]{:S(2)}) collective-permute-start(f32[64,256]{1,0:T(8,128)S(1)} %select_select_fusion.6), channel_id=1, source_target_pairs={{0,3},{1,2},{2,1},{3,0},{4,7},{5,6},{6,5},{7,4},{8,11},{9,10},{10,... | collective-permute-start | bytes 196616 | tf_op jit(solution)/shard_map/ppermute | solution.py:291
  16.3 5.2 %collective-permute-start.6 = (f32[64,256]{1,0:T(8,128)S(1)}, f32[64,256]{1,0:T(8,128)S(1)}, u32[]{:S(2)}, u32[]{:S(2)}) collective-permute-start(f32[64,256]{1,0:T(8,128)S(1)} %select_select_fusion.6), channel_id=1, source_target_pairs={{0,2},{1,3},{2,0},{3,1},{4,6},{5,7},{6,4},{7,5},{8,10},{9,11},{10,... | collective-permute-start | bytes 196616 | tf_op jit(solution)/shard_map/ppermute | solution.py:291
  16.3 5.2 %collective-permute-start.5 = (f32[64,256]{1,0:T(8,128)S(1)}, f32[64,256]{1,0:T(8,128)S(1)}, u32[]{:S(2)}, u32[]{:S(2)}) collective-permute-start(f32[64,256]{1,0:T(8,128)S(1)} %select_select_fusion.6), channel_id=1, source_target_pairs={{0,1},{1,0},{2,3},{3,2},{4,5},{5,4},{6,7},{7,6},{8,9},{9,8},{10,11... | collective-permute-start | bytes 196616 | tf_op jit(solution)/shard_map/ppermute | solution.py:291
  23.9 6.2 %collective-permute-start.10 = (f32[128,256]{1,0:T(8,128)S(1)}, f32[128,256]{1,0:T(8,128)S(1)}, u32[]{:S(2)}, u32[]{:S(2)}) collective-permute-start(f32[128,256]{1,0:T(8,128)S(1)} %pad_maximum_fusion.2), channel_id=1, source_target_pairs={{0,8},{4,12},{8,0},{12,4},{16,24},{20,28},{24,16},{28,20},{1,9},{5... | collective-permute-start | bytes 393224 | tf_op jit(solution)/shard_map/ppermute | solution.py:291
  24.7 5.4 %collective-permute-start.9 = (f32[128,256]{1,0:T(8,128)S(1)}, f32[128,256]{1,0:T(8,128)S(1)}, u32[]{:S(2)}, u32[]{:S(2)}) collective-permute-start(f32[128,256]{1,0:T(8,128)S(1)} %pad_maximum_fusion.2), channel_id=1, source_target_pairs={{0,16},{4,20},{8,24},{12,28},{16,0},{20,4},{24,8},{28,12},{1,17},{... | collective-permute-start | bytes 393224 | tf_op jit(solution)/shard_map/ppermute | solution.py:291
  26.1 5.9 %collective-permute-start.8 = (f32[128,256]{1,0:T(8,128)S(1)}, f32[128,256]{1,0:T(8,128)S(1)}, u32[]{:S(2)}, u32[]{:S(2)}) collective-permute-start(f32[128,256]{1,0:T(8,128)S(1)} %pad_maximum_fusion.2), channel_id=1, source_target_pairs={{0,24},{4,28},{8,16},{12,20},{16,8},{20,12},{24,0},{28,4},{1,25},{... | collective-permute-start | bytes 393224 | tf_op jit(solution)/shard_map/ppermute | solution.py:291
  27.5 14.7 %collective-permute-start.13 = (f32[256,256]{1,0:T(8,128)S(1)}, f32[256,256]{1,0:T(8,128)S(1)}, u32[]{:S(2)}, u32[]{:S(2)}) collective-permute-start(f32[256,256]{1,0:T(8,128)S(1)} %get-tuple-element.66), channel_id=1, source_target_pairs={{0,2},{1,3},{2,0},{3,1},{4,6},{5,7},{6,4},{7,5},{8,10},{9,11},{10,... | collective-permute-start | bytes 786440 | tf_op jit(solution)/shard_map/ppermute | solution.py:291
  32.2 1.6 %collective-permute-start.14 = (f32[256,256]{1,0:T(8,128)S(1)}, f32[256,256]{1,0:T(8,128)S(1)}, u32[]{:S(2)}, u32[]{:S(2)}) collective-permute-start(f32[256,256]{1,0:T(8,128)S(1)} %get-tuple-element.97), channel_id=1, source_target_pairs={{0,4},{4,0},{8,12},{12,8},{16,20},{20,16},{24,28},{28,24},{1,5},{5... | collective-permute-start | bytes 786440 | tf_op jit(solution)/shard_map/ppermute | solution.py:291
  32.3 27.1 %collective-permute-start.12 = (f32[1024,128]{1,0:T(8,128)S(1)}, f32[1024,128]{1,0:T(8,128)S(1)}, u32[]{:S(2)}, u32[]{:S(2)}) collective-permute-start(f32[1024,128]{1,0:T(8,128)S(1)} %broadcast_select_fusion.1), channel_id=1, source_target_pairs={{0,8},{4,12},{8,0},{12,4},{16,24},{20,28},{24,16},{28,20},{1,9},{5... | collective-permute-start | bytes 1572872 | tf_op jit(solution)/shard_map/ppermute | solution.py:291
  42.2 5.2 %collective-permute-start.17 = (f32[256,256]{1,0:T(8,128)S(1)}, f32[256,256]{1,0:T(8,128)S(1)}, u32[]{:S(2)}, u32[]{:S(2)}) collective-permute-start(f32[256,256]{1,0:T(8,128)S(1)} %get-tuple-element.73.mine1), channel_id=1, source_target_pairs={{0,4},{4,0},{8,12},{12,8},{16,20},{20,16},{24,28},{28,24},{1,5},{5... | collective-permute-start | bytes 786440 | tf_op jit(solution)/shard_map/ppermute | solution.py:291
  42.5 16.9 %collective-permute-start.11 = (f32[1024,128]{1,0:T(8,128)S(1)}, f32[1024,128]{1,0:T(8,128)S(1)}, u32[]{:S(2)}, u32[]{:S(2)}) collective-permute-start(f32[1024,128]{1,0:T(8,128)S(1)} %broadcast_select_fusion.3), channel_id=1, source_target_pairs={{0,16},{4,20},{8,24},{12,28},{16,0},{20,4},{24,8},{28,12},{1,17},{... | collective-permute-start | bytes 1572872 | tf_op jit(solution)/shard_map/ppermute | solution.py:291
  43.2 14.5 %collective-permute-start.16 = (f32[256,256]{1,0:T(8,128)S(1)}, f32[256,256]{1,0:T(8,128)S(1)}, u32[]{:S(2)}, u32[]{:S(2)}) collective-permute-start(f32[256,256]{1,0:T(8,128)S(1)} %broadcast_select_fusion.6.left), channel_id=1, source_target_pairs={{0,1},{1,0},{2,3},{3,2},{4,5},{5,4},{6,7},{7,6},{8,9},{9,8},{10,11... | collective-permute-start | bytes 786440 | tf_op jit(solution)/shard_map/ppermute | solution.py:291
  44.8 14.6 %collective-permute-start.15 = (f32[256,256]{1,0:T(8,128)S(1)}, f32[256,256]{1,0:T(8,128)S(1)}, u32[]{:S(2)}, u32[]{:S(2)}) collective-permute-start(f32[256,256]{1,0:T(8,128)S(1)} %get-tuple-element.70), channel_id=1, source_target_pairs={{0,2},{1,3},{2,0},{3,1},{4,6},{5,7},{6,4},{7,5},{8,10},{9,11},{10,... | collective-permute-start | bytes 786440 | tf_op jit(solution)/shard_map/ppermute | solution.py:291
  57.7 4.6 %copy-start.1 = (f32[2,1,256,4,1,256]{5,4,3,2,1,0:T(1,128)S(1)}, f32[2,1,256,4,1,256]{5,4,3,2,1,0:T(1,128)}, u32[]{:S(2)}) copy-start(f32[2,1,256,4,1,256]{5,4,3,2,1,0:T(1,128)} %param.1) | copy-start | bytes 6291460
  59.5 2.0 %collective-permute-start.19 = (f32[1024,128]{1,0:T(8,128)S(1)}, f32[1024,128]{1,0:T(8,128)S(1)}, u32[]{:S(2)}, u32[]{:S(2)}) collective-permute-start(f32[1024,128]{1,0:T(8,128)S(1)} %broadcast_select_fusion.mine_a), channel_id=1, source_target_pairs={{0,4},{4,0},{8,12},{12,8},{16,20},{20,16},{24,28},{28,24},{1,5},{5... | collective-permute-start | bytes 1572872 | tf_op jit(solution)/shard_map/ppermute | solution.py:291
  59.6 2.6 %collective-permute-start.20 = (f32[1024,128]{1,0:T(8,128)S(1)}, f32[1024,128]{1,0:T(8,128)S(1)}, u32[]{:S(2)}, u32[]{:S(2)}) collective-permute-start(f32[1024,128]{1,0:T(8,128)S(1)} %broadcast_select_fusion.2.mine_b), channel_id=1, source_target_pairs={{0,4},{4,0},{8,12},{12,8},{16,20},{20,16},{24,28},{28,24},{1,5},{5... | collective-permute-start | bytes 1572872 | tf_op jit(solution)/shard_map/ppermute | solution.py:291
  60.2 8.4 %collective-permute-start.18 = (f32[256,256]{1,0:T(8,128)S(1)}, f32[256,256]{1,0:T(8,128)S(1)}, u32[]{:S(2)}, u32[]{:S(2)}) collective-permute-start(f32[256,256]{1,0:T(8,128)S(1)} %broadcast_select_fusion.5.left), channel_id=1, source_target_pairs={{0,1},{1,0},{2,3},{3,2},{4,5},{5,4},{6,7},{7,6},{8,9},{9,8},{10,11... | collective-permute-start | bytes 786440 | tf_op jit(solution)/shard_map/ppermute | solution.py:291

commit v2 on v1

--- a/solution.py
+++ b/solution.py
@@ -353,10 +353,11 @@
         pos, x0, lead[0], lead[1], lead_other, lead_next,
         smem=1,
     )
-    got_a, got_b, got_left[1:], both[0], x1 = after((got_a, got_b, got_left[1:], both[0], x1))
+    got_a, got_b, both[0], x1 = after((got_a, got_b, both[0], x1))
     top_a = settle(top_a, "row", row_bits[-1], got_a)
     top_b = settle(top_b, "row", row_bits[0], got_b)
     other_a, other_b = swap(top_a, "row", 1), swap(top_b, "row", 1)
+    got_left[1:], x1 = after((got_left[1:], x1))
     both += [columns(a) for a in range(1, loc_rows)]
 
     def block(a):

time: 71.6 us -> 70 us (0.978)
  waiting for transfers between devices: 18.8 us -> 17.1 us
    ppermute x21, waiting for transfers between devices: 18.8 us -> 17.1 us  [swap(): return lax.ppermute(value, axis, [(i, i ^ bits) for i in range(size)])]
  transfers between devices with their start and end apart: 21 -> 21, of which waited for: 13 -> 12; matrix products, arithmetic and copies ran while one was open for 1% -> 1% of each run, Pallas kernels for 32% -> 33%
where the time goes in v2:
time: 70 us; the launch traced here: 69.8 us
  Pallas kernels  25.8 us (37%)
  starting transfers between devices  24.5 us (35%)
  waiting for transfers between devices  17.1 us (24%)
  local copies, waits for them, and re-layouts  1.65 us (2%)
    pallas_call x5, Pallas kernels, call(): pl.pallas_call(kernel, grid=grid, out_shape=out_shape, in_specs=specs or...  25.8 us
    ppermute x21, starting transfers between devices, swap(): return lax.ppermute(value, axis, [(i, i ^ bits) for i in range(size)])  24.5 us
    ppermute x21, waiting for transfers between devices, swap(): return lax.ppermute(value, axis, [(i, i ^ bits) for i in range(size)])  17.1 us
    unnamed x4, local copies, waits for them, and re-layouts  1.6 us
  transfers between devices with their start and end apart: 21, of which 12 were waited for; matrix products, arithmetic and copies ran while one was open for 1% of the time, Pallas kernels for 33%

profile of v2, /device:TPU:0, one launch (start us, length us, event | category | flops | bytes accessed | tf_op | source)
XLA Modules:
  0.0 69.8 jit_solution(5254046653248906263)
XLA Ops:
  0.0 1.6 %copy-done = f32[2,1,256,4,1,256]{5,4,3,2,1,0:T(1,128)S(1)} copy-done((f32[2,1,256,4,1,256]{5,4,3,2,1,0:T(1,128)S(1)}, f32[2,1,256,4,1,256]{5,4,3,2,1,0:T(1,128)}, u32[]{:S(2)}) %copy-start) | copy-done | bytes 2097176
  1.8 4.0 %collective-permute-start.2 = (f32[64,256]{1,0:T(8,128)S(1)}, f32[64,256]{1,0:T(8,128)S(1)}, u32[]{:S(2)}, u32[]{:S(2)}) collective-permute-start(f32[64,256]{1,0:T(8,128)S(1)} %get-tuple-element.104), channel_id=1, source_target_pairs={{0,24},{4,28},{8,16},{12,20},{16,8},{20,12},{24,0},{28,4},{1,25},{... | collective-permute-start | bytes 196616 | tf_op jit(solution)/shard_map/ppermute | solution.py:291
  5.7 0.5 collective-permute-start.1
  6.4 1.6 %collective-permute-done.2 = f32[64,256]{1,0:T(8,128)S(1)} collective-permute-done((f32[64,256]{1,0:T(8,128)S(1)}, f32[64,256]{1,0:T(8,128)S(1)}, u32[]{:S(2)}, u32[]{:S(2)}) %collective-permute-start.2) | collective-permute-done | bytes 65568 | tf_op jit(solution)/shard_map/ppermute | solution.py:291
  8.0 2.0 %collective-permute-done.1 = f32[64,256]{1,0:T(8,128)S(1)} collective-permute-done((f32[64,256]{1,0:T(8,128)S(1)}, f32[64,256]{1,0:T(8,128)S(1)}, u32[]{:S(2)}, u32[]{:S(2)}) %collective-permute-start.1) | collective-permute-done | bytes 65568 | tf_op jit(solution)/shard_map/ppermute | solution.py:291
  10.0 0.5 collective-permute-done
  11.0 1.6 %collective-permute-start.4 = (f32[1024,128]{1,0:T(8,128)S(1)}, f32[1024,128]{1,0:T(8,128)S(1)}, u32[]{:S(2)}, u32[]{:S(2)}) collective-permute-start(f32[1024,128]{1,0:T(8,128)S(1)} %get-tuple-element.71), channel_id=1, source_target_pairs={{0,16},{4,20},{8,24},{12,28},{16,0},{20,4},{24,8},{28,12},{1,17},{... | collective-permute-start | bytes 1572872 | tf_op jit(solution)/shard_map/ppermute | solution.py:291
  12.6 3.7 %collective-permute-start.7 = (f32[64,256]{1,0:T(8,128)S(1)}, f32[64,256]{1,0:T(8,128)S(1)}, u32[]{:S(2)}, u32[]{:S(2)}) collective-permute-start(f32[64,256]{1,0:T(8,128)S(1)} %select_select_fusion.6), channel_id=1, source_target_pairs={{0,3},{1,2},{2,1},{3,0},{4,7},{5,6},{6,5},{7,4},{8,11},{9,10},{10,... | collective-permute-start | bytes 196616 | tf_op jit(solution)/shard_map/ppermute | solution.py:291
  16.3 0.8 %collective-permute-start.5 = (f32[64,256]{1,0:T(8,128)S(1)}, f32[64,256]{1,0:T(8,128)S(1)}, u32[]{:S(2)}, u32[]{:S(2)}) collective-permute-start(f32[64,256]{1,0:T(8,128)S(1)} %select_select_fusion.6), channel_id=1, source_target_pairs={{0,1},{1,0},{2,3},{3,2},{4,5},{5,4},{6,7},{7,6},{8,9},{9,8},{10,11... | collective-permute-start | bytes 196616 | tf_op jit(solution)/shard_map/ppermute | solution.py:291
  17.0 1.8 %collective-permute-done.7 = f32[64,256]{1,0:T(8,128)S(1)} collective-permute-done((f32[64,256]{1,0:T(8,128)S(1)}, f32[64,256]{1,0:T(8,128)S(1)}, u32[]{:S(2)}, u32[]{:S(2)}) %collective-permute-start.7) | collective-permute-done | bytes 65568 | tf_op jit(solution)/shard_map/ppermute | solution.py:291
  18.8 2.6 %collective-permute-done.6 = f32[64,256]{1,0:T(8,128)S(1)} collective-permute-done((f32[64,256]{1,0:T(8,128)S(1)}, f32[64,256]{1,0:T(8,128)S(1)}, u32[]{:S(2)}, u32[]{:S(2)}) %collective-permute-start.6) | collective-permute-done | bytes 65568 | tf_op jit(solution)/shard_map/ppermute | solution.py:291
  21.4 1.4 %collective-permute-done.3 = f32[1024,128]{1,0:T(8,128)S(1)} collective-permute-done((f32[1024,128]{1,0:T(8,128)S(1)}, f32[1024,128]{1,0:T(8,128)S(1)}, u32[]{:S(2)}, u32[]{:S(2)}) %collective-permute-start.3) | collective-permute-done | bytes 524320 | tf_op jit(solution)/shard_map/ppermute | solution.py:291
  22.9 0.9 %collective-permute-done.4 = f32[1024,128]{1,0:T(8,128)S(1)} collective-permute-done((f32[1024,128]{1,0:T(8,128)S(1)}, f32[1024,128]{1,0:T(8,128)S(1)}, u32[]{:S(2)}, u32[]{:S(2)}) %collective-permute-start.4) | collective-permute-done | bytes 524320 | tf_op jit(solution)/shard_map/ppermute | solution.py:291
  23.9 0.9 %collective-permute-start.11 = (f32[128,256]{1,0:T(8,128)S(1)}, f32[128,256]{1,0:T(8,128)S(1)}, u32[]{:S(2)}, u32[]{:S(2)}) collective-permute-start(f32[128,256]{1,0:T(8,128)S(1)} %pad_maximum_fusion.2), channel_id=1, source_target_pairs={{0,8},{4,12},{8,0},{12,4},{16,24},{20,28},{24,16},{28,20},{1,9},{5... | collective-permute-start | bytes 393224 | tf_op jit(solution)/shard_map/ppermute | solution.py:291
  24.7 1.4 %collective-permute-start.10 = (f32[128,256]{1,0:T(8,128)S(1)}, f32[128,256]{1,0:T(8,128)S(1)}, u32[]{:S(2)}, u32[]{:S(2)}) collective-permute-start(f32[128,256]{1,0:T(8,128)S(1)} %pad_maximum_fusion.2), channel_id=1, source_target_pairs={{0,16},{4,20},{8,24},{12,28},{16,0},{20,4},{24,8},{28,12},{1,17},{... | collective-permute-start | bytes 393224 | tf_op jit(solution)/shard_map/ppermute | solution.py:291
  26.1 1.3 %collective-permute-start.9 = (f32[128,256]{1,0:T(8,128)S(1)}, f32[128,256]{1,0:T(8,128)S(1)}, u32[]{:S(2)}, u32[]{:S(2)}) collective-permute-start(f32[128,256]{1,0:T(8,128)S(1)} %pad_maximum_fusion.2), channel_id=1, source_target_pairs={{0,24},{4,28},{8,16},{12,20},{16,8},{20,12},{24,0},{28,4},{1,25},{... | collective-permute-start | bytes 393224 | tf_op jit(solution)/shard_map/ppermute | solution.py:291
  27.5 2.6 %collective-permute-start.8 = (f32[256,256]{1,0:T(8,128)S(1)}, f32[256,256]{1,0:T(8,128)S(1)}, u32[]{:S(2)}, u32[]{:S(2)}) collective-permute-start(f32[256,256]{1,0:T(8,128)S(1)} %get-tuple-element.62), channel_id=1, source_target_pairs={{0,2},{1,3},{2,0},{3,1},{4,6},{5,7},{6,4},{7,5},{8,10},{9,11},{10,... | collective-permute-start | bytes 786440 | tf_op jit(solution)/shard_map/ppermute | solution.py:291
  30.1 1.9 %collective-permute-done.9 = f32[128,256]{1,0:T(8,128)S(1)} collective-permute-done((f32[128,256]{1,0:T(8,128)S(1)}, f32[128,256]{1,0:T(8,128)S(1)}, u32[]{:S(2)}, u32[]{:S(2)}) %collective-permute-start.9) | collective-permute-done | bytes 131104 | tf_op jit(solution)/shard_map/ppermute | solution.py:291
  32.3 0.9 %collective-permute-start.15 = (f32[1024,128]{1,0:T(8,128)S(1)}, f32[1024,128]{1,0:T(8,128)S(1)}, u32[]{:S(2)}, u32[]{:S(2)}) collective-permute-start(f32[1024,128]{1,0:T(8,128)S(1)} %broadcast_select_fusion.1), channel_id=1, source_target_pairs={{0,8},{4,12},{8,0},{12,4},{16,24},{20,28},{24,16},{28,20},{1,9},{5... | collective-permute-start | bytes 1572872 | tf_op jit(solution)/shard_map/ppermute | solution.py:291
  33.3 0.5 collective-permute-done.12.other.other0
  33.8 8.4 %shard_map.18 = (f32[256,256]{1,0:T(8,128)S(1)}, f32[256,256]{1,0:T(8,128)S(1)}) custom-call(s32[4]{0:T(128)S(1)} %pad_add_fusion.pos, f32[256,256]{1,0:T(8,128)S(1)} %get-tuple-element.65.mine.mine0, f32[256,256]{1,0:T(8,128)S(1)} %collective-permute-done.12.other.other0), custom_call_target="tpu_custom_call" | custom-call | flops 10000000000 | bytes 4194304 | tf_op jit(solution)/shard_map/pallas_call | solution.py:264
  42.5 0.7 collective-permute-start.14
  43.2 1.6 %collective-permute-start.16 = (f32[256,256]{1,0:T(8,128)S(1)}, f32[256,256]{1,0:T(8,128)S(1)}, u32[]{:S(2)}, u32[]{:S(2)}) collective-permute-start(f32[256,256]{1,0:T(8,128)S(1)} %broadcast_select_fusion.6.left), channel_id=1, source_target_pairs={{0,1},{1,0},{2,3},{3,2},{4,5},{5,4},{6,7},{7,6},{8,9},{9,8},{10,11... | collective-permute-start | bytes 786440 | tf_op jit(solution)/shard_map/ppermute | solution.py:291
  44.8 2.6 %collective-permute-start.13 = (f32[256,256]{1,0:T(8,128)S(1)}, f32[256,256]{1,0:T(8,128)S(1)}, u32[]{:S(2)}, u32[]{:S(2)}) collective-permute-start(f32[256,256]{1,0:T(8,128)S(1)} %get-tuple-element.67), channel_id=1, source_target_pairs={{0,2},{1,3},{2,0},{3,1},{4,6},{5,7},{6,4},{7,5},{8,10},{9,11},{10,... | collective-permute-start | bytes 786440 | tf_op jit(solution)/shard_map/ppermute | solution.py:291
  47.4 10.2 %shard_map.19 = (f32[256,256]{1,0:T(8,128)S(1)}, f32[256,256]{1,0:T(8,128)S(1)}, f32[256,256]{1,0:T(8,128)S(1)}) custom-call(s32[4]{0:T(128)S(1)} %pad_add_fusion.pos, f32[256,256]{1,0:T(8,128)S(1)} %get-tuple-element.73.x0, f32[256,256]{1,0:T(8,128)S(1)} %get-tuple-element.65.mine.mine0, f32[256,256]{1,0:T(8,128)S(1)} %get-tuple-element.74.mine1, ...), custom_call_target="tpu_custom_call" | custom-call | flops 10000000000 | bytes 4194304 | tf_op jit(solution)/shard_map/pallas_call | solution.py:264
  57.9 0.5 collective-permute-start.20
  58.4 1.0 %collective-permute-done.13 = f32[256,256]{1,0:T(8,128)S(1)} collective-permute-done((f32[256,256]{1,0:T(8,128)S(1)}, f32[256,256]{1,0:T(8,128)S(1)}, u32[]{:S(2)}, u32[]{:S(2)}) %collective-permute-start.13) | collective-permute-done | bytes 262176 | tf_op jit(solution)/shard_map/ppermute | solution.py:291
  59.5 0.5 collective-permute-start.18
  60.0 0.6 collective-permute-done.20.other_b
  60.6 4.1 %shard_map.20 = (f32[4096,128]{1,0:T(8,128)}, f32[256,256]{1,0:T(8,128)S(1)}, f32[256,256]{1,0:T(8,128)S(1)}, f32[256,256]{1,0:T(8,128)S(1)}, f32[256,256]{1,0:T...) custom-call(s32[4]{0:T(128)S(1)} %pad_add_fusion.pos, ...), custom_call_target="tpu_custom_call" | custom-call | flops 1000000000 | bytes 4194304 | tf_op jit(solution)/shard_map/pallas_call | solution.py:264
  64.6 2.2 %collective-permute-done.18.right = f32[256,256]{1,0:T(8,128)S(1)} collective-permute-done((f32[256,256]{1,0:T(8,128)S(1)}, f32[256,256]{1,0:T(8,128)S(1)}, u32[]{:S(2)}, u32[]{:S(2)}) %collective-permute-start.18) | collective-permute-done | bytes 262176 | tf_op jit(solution)/shard_map/ppermute | solution.py:291
  66.8 3.0 %shard_map.21 = f32[4096,128]{1,0:T(8,128)} custom-call(s32[4]{0:T(128)S(1)} %pad_add_fusion.pos, f32[4096,128]{1,0:T(8,128)S(1)} %bitcast.6, f32[256,256]{1,0:T(8,128)S(1)} %broadcast_select_fusion.5.left, f32[256,256]{1,0:T(8,128)S(1)} %collective-permute-done.18.right, f32[256,256]{1,0:T(8,128)S(1)} %get-tuple-element.73.x0, ...), custom_call_target="tpu_custom_call", output_to_operand_aliasing={{}: (15, {})} | custom-call | flops 10000000 | bytes 4194304 | tf_op jit(solution)/shard_map/pallas_call | solution.py:264
  (34 shorter events, 1.7 us)
Async XLA Ops:
  0.0 1.6 %copy-start = (f32[2,1,256,4,1,256]{5,4,3,2,1,0:T(1,128)S(1)}, f32[2,1,256,4,1,256]{5,4,3,2,1,0:T(1,128)}, u32[]{:S(2)}) copy-start(f32[2,1,256,4,1,256]{5,4,3,2,1,0:T(1,128)} %param.1) | copy-start | bytes 6291460
  1.8 6.2 %collective-permute-start.2 = (f32[64,256]{1,0:T(8,128)S(1)}, f32[64,256]{1,0:T(8,128)S(1)}, u32[]{:S(2)}, u32[]{:S(2)}) collective-permute-start(f32[64,256]{1,0:T(8,128)S(1)} %get-tuple-element.104), channel_id=1, source_target_pairs={{0,24},{4,28},{8,16},{12,20},{16,8},{20,12},{24,0},{28,4},{1,25},{... | collective-permute-start | bytes 196616 | tf_op jit(solution)/shard_map/ppermute | solution.py:291
  5.7 4.3 %collective-permute-start.1 = (f32[64,256]{1,0:T(8,128)S(1)}, f32[64,256]{1,0:T(8,128)S(1)}, u32[]{:S(2)}, u32[]{:S(2)}) collective-permute-start(f32[64,256]{1,0:T(8,128)S(1)} %get-tuple-element.105), channel_id=1, source_target_pairs={{0,16},{4,20},{8,24},{12,28},{16,0},{20,4},{24,8},{28,12},{1,17},{... | collective-permute-start | bytes 196616 | tf_op jit(solution)/shard_map/ppermute | solution.py:291
  6.3 4.3 %collective-permute-start = (f32[64,256]{1,0:T(8,128)S(1)}, f32[64,256]{1,0:T(8,128)S(1)}, u32[]{:S(2)}, u32[]{:S(2)}) collective-permute-start(f32[64,256]{1,0:T(8,128)S(1)} %get-tuple-element.106), channel_id=1, source_target_pairs={{0,8},{4,12},{8,0},{12,4},{16,24},{20,28},{24,16},{28,20},{1,9},{5... | collective-permute-start | bytes 196616 | tf_op jit(solution)/shard_map/ppermute | solution.py:291
  10.5 12.4 %collective-permute-start.3 = (f32[1024,128]{1,0:T(8,128)S(1)}, f32[1024,128]{1,0:T(8,128)S(1)}, u32[]{:S(2)}, u32[]{:S(2)}) collective-permute-start(f32[1024,128]{1,0:T(8,128)S(1)} %get-tuple-element.69), channel_id=1, source_target_pairs={{0,8},{4,12},{8,0},{12,4},{16,24},{20,28},{24,16},{28,20},{1,9},{5... | collective-permute-start | bytes 1572872 | tf_op jit(solution)/shard_map/ppermute | solution.py:291
  11.0 12.8 %collective-permute-start.4 = (f32[1024,128]{1,0:T(8,128)S(1)}, f32[1024,128]{1,0:T(8,128)S(1)}, u32[]{:S(2)}, u32[]{:S(2)}) collective-permute-start(f32[1024,128]{1,0:T(8,128)S(1)} %get-tuple-element.71), channel_id=1, source_target_pairs={{0,16},{4,20},{8,24},{12,28},{16,0},{20,4},{24,8},{28,12},{1,17},{... | collective-permute-start | bytes 1572872 | tf_op jit(solution)/shard_map/ppermute | solution.py:291
  12.6 6.2 %collective-permute-start.7 = (f32[64,256]{1,0:T(8,128)S(1)}, f32[64,256]{1,0:T(8,128)S(1)}, u32[]{:S(2)}, u32[]{:S(2)}) collective-permute-start(f32[64,256]{1,0:T(8,128)S(1)} %select_select_fusion.6), channel_id=1, source_target_pairs={{0,3},{1,2},{2,1},{3,0},{4,7},{5,6},{6,5},{7,4},{8,11},{9,10},{10,... | collective-permute-start | bytes 196616 | tf_op jit(solution)/shard_map/ppermute | solution.py:291
  16.3 5.2 %collective-permute-start.6 = (f32[64,256]{1,0:T(8,128)S(1)}, f32[64,256]{1,0:T(8,128)S(1)}, u32[]{:S(2)}, u32[]{:S(2)}) collective-permute-start(f32[64,256]{1,0:T(8,128)S(1)} %select_select_fusion.6), channel_id=1, source_target_pairs={{0,2},{1,3},{2,0},{3,1},{4,6},{5,7},{6,4},{7,5},{8,10},{9,11},{10,... | collective-permute-start | bytes 196616 | tf_op jit(solution)/shard_map/ppermute | solution.py:291
  16.3 5.2 %collective-permute-start.5 = (f32[64,256]{1,0:T(8,128)S(1)}, f32[64,256]{1,0:T(8,128)S(1)}, u32[]{:S(2)}, u32[]{:S(2)}) collective-permute-start(f32[64,256]{1,0:T(8,128)S(1)} %select_select_fusion.6), channel_id=1, source_target_pairs={{0,1},{1,0},{2,3},{3,2},{4,5},{5,4},{6,7},{7,6},{8,9},{9,8},{10,11... | collective-permute-start | bytes 196616 | tf_op jit(solution)/shard_map/ppermute | solution.py:291
  23.9 6.2 %collective-permute-start.11 = (f32[128,256]{1,0:T(8,128)S(1)}, f32[128,256]{1,0:T(8,128)S(1)}, u32[]{:S(2)}, u32[]{:S(2)}) collective-permute-start(f32[128,256]{1,0:T(8,128)S(1)} %pad_maximum_fusion.2), channel_id=1, source_target_pairs={{0,8},{4,12},{8,0},{12,4},{16,24},{20,28},{24,16},{28,20},{1,9},{5... | collective-permute-start | bytes 393224 | tf_op jit(solution)/shard_map/ppermute | solution.py:291
  24.7 5.4 %collective-permute-start.10 = (f32[128,256]{1,0:T(8,128)S(1)}, f32[128,256]{1,0:T(8,128)S(1)}, u32[]{:S(2)}, u32[]{:S(2)}) collective-permute-start(f32[128,256]{1,0:T(8,128)S(1)} %pad_maximum_fusion.2), channel_id=1, source_target_pairs={{0,16},{4,20},{8,24},{12,28},{16,0},{20,4},{24,8},{28,12},{1,17},{... | collective-permute-start | bytes 393224 | tf_op jit(solution)/shard_map/ppermute | solution.py:291
  26.1 5.9 %collective-permute-start.9 = (f32[128,256]{1,0:T(8,128)S(1)}, f32[128,256]{1,0:T(8,128)S(1)}, u32[]{:S(2)}, u32[]{:S(2)}) collective-permute-start(f32[128,256]{1,0:T(8,128)S(1)} %pad_maximum_fusion.2), channel_id=1, source_target_pairs={{0,24},{4,28},{8,16},{12,20},{16,8},{20,12},{24,0},{28,4},{1,25},{... | collective-permute-start | bytes 393224 | tf_op jit(solution)/shard_map/ppermute | solution.py:291
  27.5 14.7 %collective-permute-start.8 = (f32[256,256]{1,0:T(8,128)S(1)}, f32[256,256]{1,0:T(8,128)S(1)}, u32[]{:S(2)}, u32[]{:S(2)}) collective-permute-start(f32[256,256]{1,0:T(8,128)S(1)} %get-tuple-element.62), channel_id=1, source_target_pairs={{0,2},{1,3},{2,0},{3,1},{4,6},{5,7},{6,4},{7,5},{8,10},{9,11},{10,... | collective-permute-start | bytes 786440 | tf_op jit(solution)/shard_map/ppermute | solution.py:291
  32.2 1.6 %collective-permute-start.12 = (f32[256,256]{1,0:T(8,128)S(1)}, f32[256,256]{1,0:T(8,128)S(1)}, u32[]{:S(2)}, u32[]{:S(2)}) collective-permute-start(f32[256,256]{1,0:T(8,128)S(1)} %get-tuple-element.99), channel_id=1, source_target_pairs={{0,4},{4,0},{8,12},{12,8},{16,20},{20,16},{24,28},{28,24},{1,5},{5... | collective-permute-start | bytes 786440 | tf_op jit(solution)/shard_map/ppermute | solution.py:291
  32.3 25.4 %collective-permute-start.15 = (f32[1024,128]{1,0:T(8,128)S(1)}, f32[1024,128]{1,0:T(8,128)S(1)}, u32[]{:S(2)}, u32[]{:S(2)}) collective-permute-start(f32[1024,128]{1,0:T(8,128)S(1)} %broadcast_select_fusion.1), channel_id=1, source_target_pairs={{0,8},{4,12},{8,0},{12,4},{16,24},{20,28},{24,16},{28,20},{1,9},{5... | collective-permute-start | bytes 1572872 | tf_op jit(solution)/shard_map/ppermute | solution.py:291
  42.2 5.2 %collective-permute-start.17 = (f32[256,256]{1,0:T(8,128)S(1)}, f32[256,256]{1,0:T(8,128)S(1)}, u32[]{:S(2)}, u32[]{:S(2)}) collective-permute-start(f32[256,256]{1,0:T(8,128)S(1)} %get-tuple-element.74.mine1), channel_id=1, source_target_pairs={{0,4},{4,0},{8,12},{12,8},{16,20},{20,16},{24,28},{28,24},{1,5},{5... | collective-permute-start | bytes 786440 | tf_op jit(solution)/shard_map/ppermute | solution.py:291
  42.5 15.3 %collective-permute-start.14 = (f32[1024,128]{1,0:T(8,128)S(1)}, f32[1024,128]{1,0:T(8,128)S(1)}, u32[]{:S(2)}, u32[]{:S(2)}) collective-permute-start(f32[1024,128]{1,0:T(8,128)S(1)} %broadcast_select_fusion.3), channel_id=1, source_target_pairs={{0,16},{4,20},{8,24},{12,28},{16,0},{20,4},{24,8},{28,12},{1,17},{... | collective-permute-start | bytes 1572872 | tf_op jit(solution)/shard_map/ppermute | solution.py:291
  43.2 14.5 %collective-permute-start.16 = (f32[256,256]{1,0:T(8,128)S(1)}, f32[256,256]{1,0:T(8,128)S(1)}, u32[]{:S(2)}, u32[]{:S(2)}) collective-permute-start(f32[256,256]{1,0:T(8,128)S(1)} %broadcast_select_fusion.6.left), channel_id=1, source_target_pairs={{0,1},{1,0},{2,3},{3,2},{4,5},{5,4},{6,7},{7,6},{8,9},{9,8},{10,11... | collective-permute-start | bytes 786440 | tf_op jit(solution)/shard_map/ppermute | solution.py:291
  44.8 14.6 %collective-permute-start.13 = (f32[256,256]{1,0:T(8,128)S(1)}, f32[256,256]{1,0:T(8,128)S(1)}, u32[]{:S(2)}, u32[]{:S(2)}) collective-permute-start(f32[256,256]{1,0:T(8,128)S(1)} %get-tuple-element.67), channel_id=1, source_target_pairs={{0,2},{1,3},{2,0},{3,1},{4,6},{5,7},{6,4},{7,5},{8,10},{9,11},{10,... | collective-permute-start | bytes 786440 | tf_op jit(solution)/shard_map/ppermute | solution.py:291
  57.7 2.9 %copy-start.1 = (f32[2,1,256,4,1,256]{5,4,3,2,1,0:T(1,128)S(1)}, f32[2,1,256,4,1,256]{5,4,3,2,1,0:T(1,128)}, u32[]{:S(2)}) copy-start(f32[2,1,256,4,1,256]{5,4,3,2,1,0:T(1,128)} %param.1) | copy-start | bytes 6291460
  57.9 2.1 %collective-permute-start.19 = (f32[1024,128]{1,0:T(8,128)S(1)}, f32[1024,128]{1,0:T(8,128)S(1)}, u32[]{:S(2)}, u32[]{:S(2)}) collective-permute-start(f32[1024,128]{1,0:T(8,128)S(1)} %broadcast_select_fusion.mine_a), channel_id=1, source_target_pairs={{0,4},{4,0},{8,12},{12,8},{16,20},{20,16},{24,28},{28,24},{1,5},{5... | collective-permute-start | bytes 1572872 | tf_op jit(solution)/shard_map/ppermute | solution.py:291
  57.9 2.6 %collective-permute-start.20 = (f32[1024,128]{1,0:T(8,128)S(1)}, f32[1024,128]{1,0:T(8,128)S(1)}, u32[]{:S(2)}, u32[]{:S(2)}) collective-permute-start(f32[1024,128]{1,0:T(8,128)S(1)} %broadcast_select_fusion.2.mine_b), channel_id=1, source_target_pairs={{0,4},{4,0},{8,12},{12,8},{16,20},{20,16},{24,28},{28,24},{1,5},{5... | collective-permute-start | bytes 1572872 | tf_op jit(solution)/shard_map/ppermute | solution.py:291
  59.5 7.4 %collective-permute-start.18 = (f32[256,256]{1,0:T(8,128)S(1)}, f32[256,256]{1,0:T(8,128)S(1)}, u32[]{:S(2)}, u32[]{:S(2)}) collective-permute-start(f32[256,256]{1,0:T(8,128)S(1)} %broadcast_select_fusion.5.left), channel_id=1, source_target_pairs={{0,1},{1,0},{2,3},{3,2},{4,5},{5,4},{6,7},{7,6},{8,9},{9,8},{10,11... | collective-permute-start | bytes 786440 | tf_op jit(solution)/shard_map/ppermute | solution.py:291
